TPU v7x, 32 devices: a whole 2x2x4 slice. The times are simulated.
32 devices in a mesh: groups: 2 (over x), tile: 8 (over z, y), example: 2 (over core).
Axes of the slice: x: 2, y: 2, z: 4, core: 2. Of those that a mesh axis runs over, the one named last changes fastest.
Arguments:
- features: bfloat16 [4096, 8192], P(('groups', 'example'), 'tile'), parts along dimension 0
- tile_lists: int32 [272, 3], P('groups'), parts along dimension 0, may hold values from 0 to 15, as said below
- noise_tiles: float32 [544, 512, 512], P(('groups', 'tile'), 'example'), parts along dimension 0, may hold values from -6 to 6
Outputs:
- covariance: float32 [544, 512, 512], P(('groups', 'tile'), 'example'), parts along dimension 0
There are 2 independent parts, one for each index of `groups`. A program takes and returns all parts, laid end to end along the dimension named above; each array names one. Nothing has to cross between parts.
Inputs may be any that keep to these rules, and one draw needn't show every extreme that they name: `tile_lists`: every tile (i, j) with 0 <= j <= i < 16 appears once, in an order drawn from the seed; owners lie in 0 to 7, no owner has more than 34 tiles and some owner has exactly 34.
All inputs are finite; a program needn't handle non-finite values.
Results may differ from a plain program's by a relative error of at most 0.0023.
Values may be sent and summed in bfloat16 or wider, within the bound.
No kernel may reach another device: no remote copies, remote signals or barrier semaphores. Data moves between devices by JAX's collectives and lax.ppermute only.
A program may use at most 192 MiB of HBM per device.

v0:
```python
import functools
import math

import jax
import jax.numpy as jnp
import numpy as np
from jax import lax
from jax.experimental import pallas as pl
from jax.experimental.pallas import tpu as pltpu
from jax.sharding import PartitionSpec as P

F = 8192
VMEM = 63 * 1024 * 1024
CORES = [(0, 1), (1, 0)]

SLOTS = 7


def partner(chip, along):
    z, y = chip // 2, chip % 2
    if along == "y":
        return 2 * z + 1 - y
    return 2 * ((z ^ 1) if along == "z" else 3 - z) + y


def is_end(chip):
    return chip // 2 in (0, 3)


def z_core(k):
    return ((k + 1) // 2) % 2


def slot_pairs(k):
    c = z_core(k)
    pairs = []
    for chip in range(8):
        pairs.append((2 * chip + c, 2 * partner(chip, "z") + c))
        pairs.append((2 * chip + 1 - c, 2 * partner(chip, "y" if is_end(chip) else "m") + 1 - c))
    return pairs


Y_SWAP = [(chip, partner(chip, "y")) for chip in range(8)]


def slot_table(tile_lists, owner, slots):
    owners = tile_lists[:, 2]
    entries = tile_lists.shape[0]
    position = jnp.arange(entries, dtype=jnp.int32)
    mine = owners == owner
    earlier = (position[None, :] < position[:, None]) & mine[None, :]
    ranks = jnp.sum(earlier.astype(jnp.int32), axis=1)
    matches = (
        mine[None, :] & (ranks[None, :] == jnp.arange(slots, dtype=jnp.int32)[:, None])
    ).astype(jnp.int32)
    living = jnp.sum(matches, axis=1)
    first = jnp.sum(matches * tile_lists[None, :, 0], axis=1)
    second = jnp.sum(matches * tile_lists[None, :, 1], axis=1)
    return (first, second, living)


AHEAD, BEHIND, CLEAR = 6, 4, 4

EVENTS = ["own", 0, 1, 2, 3, 4, 5, 6]


def numbers(stripes):
    devices = range(16)
    got = {d: [] for d in devices}
    for k in range(SLOTS):
        sent = {d: (d if k < 2 else got[d][k - 2]) for d in devices}
        for a, b in slot_pairs(k):
            got[b].append(sent[a])
    table = np.zeros((16, 2 * len(EVENTS) + stripes), np.int32)
    for d in devices:
        row = table[d]
        places = row[2 * len(EVENTS) :]
        for k, event in enumerate(EVENTS):
            for j, who in enumerate((d, d ^ 1)):
                if event == "own":
                    stripe = who
                else:
                    stripe = got[who][event]
                row[2 * k + j] = stripe
                places[stripe] = 2 * k + j
        assert sorted(row[: 2 * len(EVENTS)]) == list(range(stripes))
    return table


def call(kernel, name, operands, scalars, results, scratch, aliases, after=(), space=pltpu.HBM):
    hbm = pl.BlockSpec(memory_space=space)
    operands = [*operands, *after]
    return pl.pallas_call(
        kernel,
        in_specs=[pl.BlockSpec(memory_space=pltpu.SMEM)] * scalars + [hbm] * (len(operands) - scalars),
        out_specs=[hbm] * len(results),
        out_shape=[jax.ShapeDtypeStruct(shape, dtype) for shape, dtype in results],
        scratch_shapes=scratch,
        input_output_aliases=aliases,
        compiler_params=pltpu.CompilerParams(vmem_limit_bytes=VMEM),
        cost_estimate=pl.CostEstimate(flops=1024, bytes_accessed=1024, transcendentals=0),
        name=name,
    )(*operands)


def keep(arrays, after):
    return call(
        lambda *_: None,
        "keep",
        arrays,
        0,
        [(x.shape, x.dtype) for x in arrays],
        [],
        {k: k for k in range(len(arrays))},
        after,
    )


def own_kernel(place, mine, other, *rest):
    whole, room, arrive, leave = rest[-4:]
    core = place[0]
    rows, stripe = other.shape
    pieces = arrive.shape[0] // 2
    part = rows // pieces
    column = pl.ds(pl.multiple_of(core * stripe, stripe), stripe)
    copies = []
    for k, side in enumerate((core, 1 - core)):
        for r in range(pieces):
            at = pl.ds(r * part, part)
            target = pl.ds(pl.multiple_of(side * rows + r * part, part), part)
            source = mine.at[at, column] if k == 0 else other.at[at]
            spot = pieces * k + r
            copies.append((
                pltpu.make_async_copy(source, room.at[k, at], arrive.at[spot]),
                pltpu.make_async_copy(room.at[k, at], whole.at[target], leave.at[spot]),
            ))
    for into, _ in copies:
        into.start()
    for into, outof in copies:
        into.wait()
        outof.start()
    for _, outof in copies:
        outof.wait()


def own_stripe(place, mine, other, after):
    rows, stripe = other.shape
    return call(
        own_kernel,
        "own",
        [place, mine, other],
        1,
        [((2 * rows, stripe), jnp.bfloat16)],
        [
            pltpu.VMEM((2, rows, stripe), jnp.bfloat16),
            pltpu.SemaphoreType.DMA((4,)),
            pltpu.SemaphoreType.DMA((4,)),
        ],
        {},
        after,
        pl.ANY,
    )[0]


def unpack_kernel(event, meta, inverse, raw, *rest):
    held, *halves = rest[-9:-6]
    taken, given, scales, arrive, leave, wide = rest[-6:]
    depth = held.shape[1]
    pieces = arrive.shape[0]
    part = depth // pieces
    place = meta[2 * event]

    def rows(r):
        return pl.ds(r * part, part)

    def into(r):
        return [
            pltpu.make_async_copy(raw.at[rows(r)], taken.at[rows(r)], arrive.at[r]),
            pltpu.make_async_copy(inverse.at[rows(r)], scales.at[rows(r)], wide.at[r]),
        ]

    def outof(r):
        half = pieces // 2
        return [
            pltpu.make_async_copy(given.at[rows(r)], halves[r // half].at[rows(r % half)], leave.at[2 * r]),
            pltpu.make_async_copy(given.at[rows(r)], held.at[place, rows(r)], leave.at[2 * r + 1]),
        ]

    for r in range(pieces):
        for copy in into(r):
            copy.start()
    for r in range(pieces):
        for copy in into(r):
            copy.wait()
        given[rows(r)] = (taken[rows(r)].astype(jnp.float32) * scales[rows(r), :1]).astype(jnp.bfloat16)
        for copy in outof(r):
            copy.start()
    for r in range(pieces):
        for copy in outof(r):
            copy.wait()


def unpack(event, raw, meta, inverse, shape, held):
    stripes, depth, stripe = shape
    half = ((depth // 2, stripe), jnp.bfloat16)
    pieces = 8
    given, aliases = [meta, inverse, raw], {}
    if held is not None:
        aliases[len(given)] = 0
        given.append(held)
    held, *halves = call(
        functools.partial(unpack_kernel, event),
        "unpack",
        given,
        1,
        [(shape, jnp.bfloat16), half, half],
        [
            pltpu.VMEM((depth, stripe), jnp.bfloat16),
            pltpu.VMEM((depth, stripe), jnp.bfloat16),
            pltpu.VMEM(inverse.shape, jnp.float32),
            pltpu.SemaphoreType.DMA((pieces,)),
            pltpu.SemaphoreType.DMA((2 * pieces,)),
            pltpu.SemaphoreType.DMA((pieces,)),
        ],
        aliases,
    )
    return held, halves


def dot(left, right):
    return lax.dot_general(left, right, (((0,), (0,)), ((), ())), preferred_element_type=jnp.float32)


def stage_kernel(cov_scale, stage, given, last, meta, lefts, rights, slots, spans, noise, *rest):
    given = rest[:given]
    held, out, lbuf, rbuf, noises, outs, zeros, arrive, leave, streamed, noised, stored, fill = rest[-13:]
    _, height, stripe = out.shape
    depth = held.shape[1]
    rows = depth // 2
    ahead, behind = noises.shape[0], outs.shape[0]
    dead, here, begin, middle, end = spans[0], spans[1], *(spans[2 + 2 * stage + k] for k in range(3))
    place = meta[stage]
    columns = pl.ds(pl.multiple_of(here * height, height), height)
    sides = [pl.ds(h * rows, rows) for h in range(2)]
    sources = given or [held.at[place, side] for side in sides]
    into = [pltpu.make_async_copy(sources[h], rbuf.at[0, sides[h]], arrive.at[h]) for h in range(2)]
    outof = [pltpu.make_async_copy(rbuf.at[0, side], held.at[place, side], leave.at[h]) for h, side in enumerate(sides)]

    def clear(e):
        return pltpu.make_async_copy(zeros, out.at[slots[e]], fill)

    def by_row(e):
        return e < middle

    def by_column(e):
        return (e >= middle) & (lefts[e] != rights[e])

    def fetch(e, step):
        b = lax.rem(e - begin, ahead)
        step(pltpu.make_async_copy(noise.at[slots[e]], noises.at[b], noised.at[b]))
        right = pltpu.make_async_copy(held.at[rights[e]], rbuf.at[1 + b], streamed.at[b])
        left = pltpu.make_async_copy(held.at[lefts[e], :, columns], lbuf.at[1 + b], streamed.at[b])
        pl.when(by_row(e))(lambda: step(right))
        pl.when(by_column(e))(lambda: step(left))

    def store(e):
        o = lax.rem(e - begin, behind)
        return pltpu.make_async_copy(outs.at[o], out.at[slots[e]], stored.at[o])

    def one_tile(e):
        b, o = lax.rem(e - begin, ahead), lax.rem(e - begin, behind)
        fetch(e, lambda copy: copy.wait())
        pl.when(e - begin >= behind)(lambda: store(e).wait())
        left = lbuf[jnp.where(by_column(e), 1 + b, 0)]
        right = rbuf[jnp.where(by_row(e), 1 + b, 0)]
        outs[o] = cov_scale * dot(left, right) + noises[b]
        store(e).start()
        pl.when(e + ahead < end)(lambda: fetch(e + ahead, lambda copy: copy.start()))

    if stage == CLEAR:

        @pl.when(dead > 0)
        def _():
            zeros[...] = jnp.zeros_like(zeros)
            pl.loop(0, dead)(lambda e: clear(e).start())

    @pl.when((end > begin) | (len(given) > 0 and not last))
    def _():
        for copy in into:
            copy.start()
        pl.loop(begin, jnp.minimum(begin + ahead, end))(lambda e: fetch(e, lambda copy: copy.start()))
        for copy in into:
            copy.wait()
        if given and not last:
            for copy in outof:
                copy.start()

        @pl.when(end > begin)
        def _():
            lbuf[0] = rbuf[0, :, columns]
            pl.loop(begin, end)(one_tile)
            pl.loop(jnp.maximum(end - behind, begin), end)(lambda e: store(e).wait())

        if given and not last:
            for copy in outof:
                copy.wait()

    if stage == CLEAR:
        pl.when(dead > 0)(lambda: pl.loop(0, dead)(lambda e: clear(e).wait()))


def run_stage(cov_scale, stage, halves, meta, table, spans, noise, held, out):
    slots, height, stripe = noise.shape
    stripes, depth = held.shape[:2]
    given = [meta, *table, spans, noise, *halves, held]
    aliases = {len(given) - 1: 0}
    if out is not None:
        aliases[len(given)] = 1
        given.append(out)
    return call(
        functools.partial(stage_kernel, cov_scale, stage, len(halves), stage == 2 * len(EVENTS) - 1),
        "stage",
        given,
        5,
        [(held.shape, jnp.bfloat16), (noise.shape, jnp.float32)],
        [
            pltpu.VMEM((1 + AHEAD, depth, height), jnp.bfloat16),
            pltpu.VMEM((1 + AHEAD, depth, stripe), jnp.bfloat16),
            pltpu.VMEM((AHEAD, height, stripe), jnp.float32),
            pltpu.VMEM((BEHIND, height, stripe), jnp.float32),
            pltpu.VMEM((height, stripe), jnp.float32),
            pltpu.SemaphoreType.DMA((2,)),
            pltpu.SemaphoreType.DMA((2,)),
            pltpu.SemaphoreType.DMA((AHEAD,)),
            pltpu.SemaphoreType.DMA((AHEAD,)),
            pltpu.SemaphoreType.DMA((BEHIND,)),
            pltpu.SemaphoreType.DMA(()),
        ],
        aliases,
    )


def plain_kernel(cov_scale, lefts, rights, slots, spans, noise, held, out, zeros, fill):
    _, height, stripe = out.shape
    depth = held.shape[1]
    dead, here, end = spans[0], spans[1], spans[4]

    def clear(e):
        return pltpu.make_async_copy(zeros, out.at[slots[e]], fill)

    def one_tile(l, r, n, o):
        o[0] = cov_scale * dot(l[0], r[0]) + n[0]

    @pl.when(dead > 0)
    def _():
        zeros[...] = jnp.zeros_like(zeros)
        pl.loop(0, dead)(lambda e: clear(e).start())
        pl.loop(0, dead)(lambda e: clear(e).wait())

    tile = pl.BlockSpec((1, height, stripe), lambda e: (slots[dead + e], 0, 0))
    left = pl.BlockSpec((1, depth, height), lambda e: (lefts[dead + e], 0, here))
    right = pl.BlockSpec((1, depth, stripe), lambda e: (rights[dead + e], 0, 0))
    pl.when(end > dead)(
        lambda: pltpu.emit_pipeline(
            one_tile, grid=(end - dead,), in_specs=[left, right, tile], out_specs=[tile]
        )(held, held, noise, out)
    )


def schedule(first, second, living, stage_of, stages, core):
    slots = first.shape[0]
    look = lambda index: jnp.sum(
        jnp.where(index[:, None] == jnp.arange(stage_of.shape[0])[None, :], stage_of[None, :], 0), axis=1
    )
    one, two = look(first), look(second)
    stage = jnp.where(living > 0, 2 * jnp.maximum(one, two) + (two >= one).astype(jnp.int32), -1)
    position = jnp.arange(slots, dtype=jnp.int32)
    key = ((stage + 1) * 64 + second) * slots + position
    rank = jnp.sum((key[None, :] < key[:, None]).astype(jnp.int32), axis=1)
    pick = (rank[None, :] == position[:, None]).astype(jnp.int32)
    put = lambda values: jnp.sum(pick * values[None, :], axis=1)
    table = (put(first), put(second), put(position))
    bounds = jnp.sum((stage[None, :] < jnp.arange(2 * stages + 1)[:, None]).astype(jnp.int32), axis=1)
    return table, jnp.concatenate([bounds[:1], core.reshape(1), bounds]).astype(jnp.int32)


def grid_body(features, tile_lists, noise_tiles):
    slots, height, stripe = noise_tiles.shape
    rows = features.shape[0]
    chips = lax.axis_size("tile")
    stripes = features.shape[1] * chips // stripe
    shape = (stripes, 2 * rows, stripe)
    chip = lax.axis_index("tile")
    core = lax.axis_index("example").astype(jnp.int32)
    cov_scale = F / math.sqrt(rows * lax.axis_size("example"))
    slot = lambda k, x: lax.ppermute(x, ("tile", "example"), slot_pairs(k))
    swap = lambda x: lax.ppermute(x, "example", CORES)

    joint = lambda x, pairs: lax.ppermute(x, ("tile", "example"), pairs)
    place = core.reshape(1)

    rows_other = swap(lax.dynamic_slice_in_dim(features, (1 - core) * stripe, stripe, 1))
    values = features.astype(jnp.float32)
    squares = jnp.sum(values * values, axis=1)
    squares_y = lax.ppermute(squares, "tile", Y_SWAP)
    raw = own_stripe(place, features, rows_other, [squares_y])
    first_sent = slot(0, raw)
    squares = squares + squares_y
    squares_other = swap(squares)
    both = jnp.where(core == 0, jnp.stack([squares, squares_other]), jnp.stack([squares_other, squares]))
    norms = both
    for k in (1, 2, 3):
        source = lambda c: 2 * c + (0 if k > 1 and not is_end(c) else 1)
        norms = norms + joint(both, [(source(c), 2 * (c ^ (2 * k)) + 1) for c in range(chips)])
    [later] = keep([raw], [norms])
    norms = jnp.where(core == 1, norms, swap(norms)).reshape(2 * rows)
    inverse = 1.0 / jnp.maximum(jnp.sqrt(norms), math.sqrt(2.0 * F))
    inverse = jnp.broadcast_to(inverse[:, None], (2 * rows, 128))

    meta = lax.dynamic_index_in_dim(jnp.asarray(numbers(stripes)), 2 * chip + core, 0, keepdims=False)
    first, second, living = slot_table(tile_lists, chip, slots)
    table, spans = schedule(first, second, living, meta[2 * len(EVENTS) :], 2 * len(EVENTS), core)

    come = [first_sent, slot(1, later)]
    held = out = None
    for k, event in enumerate(EVENTS):
        raw = later if event == "own" else come[event]
        if event in (0, 2, 4):
            come.append(slot(event + 2, raw))
        held, halves = unpack(k, raw, meta, inverse, shape, held)
        halves = [swap(x) for x in halves]
        held, out = run_stage(cov_scale, 2 * k, [], meta, table, spans, noise_tiles, held, out)
        held, out = run_stage(cov_scale, 2 * k + 1, halves, meta, table, spans, noise_tiles, held, out)
        if event == "own":
            [come[0]] = keep([come[0]], [out])
        if event in (1, 3):
            [come[event]] = keep([come[event]], [out])
            come.append(slot(event + 2, come[event]))
    return out


def plain_body(features, tile_lists, noise_tiles):
    slots, height, stripe = noise_tiles.shape
    rows = features.shape[0]
    chips = lax.axis_size("tile")
    stripes = features.shape[1] * chips // stripe
    core = lax.axis_index("example").astype(jnp.int32)
    cov_scale = F / math.sqrt(rows * lax.axis_size("example"))
    values = features.astype(jnp.float32)
    norms = lax.psum(jnp.sum(values * values, axis=1), "tile")
    inverse = (1.0 / jnp.maximum(jnp.sqrt(norms), math.sqrt(2.0 * F)))[:, None]
    scaled = (values * inverse).astype(jnp.bfloat16)
    wide = lax.all_gather(lax.all_gather(scaled, "tile", axis=1, tiled=True), "example", axis=0, tiled=True)
    held = wide.reshape(2 * rows, stripes, stripe).transpose(1, 0, 2)
    first, second, living = slot_table(tile_lists, lax.axis_index("tile"), slots)
    table, spans = schedule(first, second, living, jnp.zeros((stripes,), jnp.int32), 1, core)
    return call(
        functools.partial(plain_kernel, cov_scale),
        "plain",
        [*table, spans, noise_tiles, held],
        4,
        [(noise_tiles.shape, jnp.float32)],
        [pltpu.VMEM((height, stripe), jnp.float32), pltpu.SemaphoreType.DMA(())],
        {},
    )[0]


def body(features, tile_lists, noise_tiles):
    if lax.axis_size("tile") == 8 and features.shape[1] == 2 * noise_tiles.shape[2]:
        return grid_body(features, tile_lists, noise_tiles)
    return plain_body(features, tile_lists, noise_tiles)


def solution(mesh):
    placed = (
        P(("groups", "example"), "tile"),
        P("groups", None),
        P(("groups", "tile"), "example", None),
    )
    return jax.shard_map(
        body,
        mesh=mesh,
        in_specs=placed,
        out_specs=P(("groups", "tile"), "example", None),
        check_vma=False,
    )
```

profile of v0, /device:TPU:19, one launch (start us, length us, event | category | flops | bytes accessed | tf_op | source)
XLA Modules:
  0.0 198.7 jit_solution(7867655042415142471)
XLA Ops:
  7.6 2.4 %own.1.__0_ = bf16[2048,512]{1,0:T(8,128)(2,1)} custom-call(s32[1]{0:T(128)} %bitcast.4.place, bf16[1024,1024]{1,0:T(8,128)(2,1)} %mine.1, bf16[1024,512]{1,0:T(8,128)(2,1)} %copy-done, f32[1024]{0:T(1024)} %copy-done.2), custom_call_target="tpu_custom_call" | custom-call | flops 1024 | bytes 1024 | tf_op jit(solution)/shard_map/own/pallas_call | solution.py:93
  11.7 2.6 %collective-permute-start.1 = (f32[1024]{0:T(1024)S(1)}, f32[1024]{0:T(1024)S(1)}, u32[]{:S(2)}, u32[]{:S(2)}) collective-permute-start(f32[1024]{0:T(1024)S(1)} %add.79), channel_id=1, source_target_pairs={{0,1},{1,0},{2,3},{3,2},{4,5},{5,4},{6,7},{7,6},{8,9},{9,8},{10,11... | collective-permute-start | bytes 12296 | tf_op jit(solution)/shard_map/ppermute | solution.py:397
  20.1 2.6 %collective-permute-done.3 = f32[2,1024]{1,0:T(2,128)S(1)} collective-permute-done((f32[2,1024]{1,0:T(2,128)S(1)}, f32[2,1024]{1,0:T(2,128)S(1)}, u32[]{:S(2)}, u32[]{:S(2)}) %collective-permute-start.3) | collective-permute-done | bytes 8224 | tf_op jit(solution)/shard_map/ppermute | solution.py:399
  26.6 9.4 %collective-permute-done.7.__0_ = bf16[2048,512]{1,0:T(8,128)(2,1)} collective-permute-done((bf16[2048,512]{1,0:T(8,128)(2,1)}, bf16[2048,512]{1,0:T(8,128)(2,1)}, u32[]{:S(2)}, u32[]{:S(2)}) %collective-permute-start.7) | collective-permute-done | bytes 2097184 | tf_op jit(solution)/shard_map/ppermute | solution.py:396
  38.2 4.0 %unpack.8 = (bf16[16,2048,512]{2,1,0:T(8,128)(2,1)}, bf16[1024,512]{1,0:T(8,128)(2,1)}, bf16[1024,512]{1,0:T(8,128)(2,1)}) custom-call(s32[32]{0:T(128)} %get-tuple-element.126.meta, f32[2048,128]{1,0:T(8,128)} %broadcast_in_dim.28.inverse, bf16[2048,512]{1,0:T(8,128)(2,1)} %keep.4.raw), custom_call_target="tpu_custom_call" | custom-call | flops 1024 | bytes 1024 | tf_op jit(solution)/shard_map/unpack/pallas_call | solution.py:93
  47.9 4.4 %stage.17 = (bf16[16,2048,512]{2,1,0:T(8,128)(2,1)}, f32[34,256,512]{2,1,0:T(8,128)}) custom-call(s32[32]{0:T(128)} %get-tuple-element.126.meta, s32[34]{0:T(128)} %get-tuple-element.120.lefts, s32[34]{0:T(128)} %get-tuple-element.119.rights, s32[34]{0:T(128)} %get-tuple-element.118.slots, ...), custom_call_target="tpu_custom_call", output_to_operand_aliasing={{0}: (8, {}), {1}: (9, {})} | custom-call | flops 1024 | bytes 1024 | tf_op jit(solution)/shard_map/stage/pallas_call | solution.py:93
  52.4 4.0 %unpack.9 = (bf16[16,2048,512]{2,1,0:T(8,128)(2,1)}, bf16[1024,512]{1,0:T(8,128)(2,1)}, bf16[1024,512]{1,0:T(8,128)(2,1)}) custom-call(s32[32]{0:T(128)} %get-tuple-element.126.meta, f32[2048,128]{1,0:T(8,128)} %broadcast_in_dim.28.inverse, bf16[2048,512]{1,0:T(8,128)(2,1)} %keep.5.raw, ...), custom_call_target="tpu_custom_call", output_to_operand_aliasing={{0}: (3, {})} | custom-call | flops 1024 | bytes 1024 | tf_op jit(solution)/shard_map/unpack/pallas_call | solution.py:93
  57.2 4.2 %collective-permute-start.10 = (bf16[2048,512]{1,0:T(8,128)(2,1)}, bf16[2048,512]{1,0:T(8,128)(2,1)}, u32[]{:S(2)}, u32[]{:S(2)}) collective-permute-start(bf16[2048,512]{1,0:T(8,128)(2,1)} %keep.5.raw), channel_id=1, source_target_pairs={{1,5},{0,2},{3,7},{2,0},{5,1},{4,8},{7,3},{6,10},{9,13},{8,4},{11,... | collective-permute-start | bytes 6291464 | tf_op jit(solution)/shard_map/ppermute | solution.py:396
  61.4 4.4 %stage.18 = (bf16[16,2048,512]{2,1,0:T(8,128)(2,1)}, f32[34,256,512]{2,1,0:T(8,128)}) custom-call(s32[32]{0:T(128)} %get-tuple-element.126.meta, s32[34]{0:T(128)} %get-tuple-element.120.lefts, s32[34]{0:T(128)} %get-tuple-element.119.rights, s32[34]{0:T(128)} %get-tuple-element.118.slots, ...), custom_call_target="tpu_custom_call", output_to_operand_aliasing={{0}: (6, {}), {1}: (7, {})} | custom-call | flops 1024 | bytes 1024 | tf_op jit(solution)/shard_map/stage/pallas_call | solution.py:93
  65.8 3.8 %stage.19 = (bf16[16,2048,512]{2,1,0:T(8,128)(2,1)}, f32[34,256,512]{2,1,0:T(8,128)}) custom-call(s32[32]{0:T(128)} %get-tuple-element.126.meta, s32[34]{0:T(128)} %get-tuple-element.120.lefts, s32[34]{0:T(128)} %get-tuple-element.119.rights, s32[34]{0:T(128)} %get-tuple-element.118.slots, ...), custom_call_target="tpu_custom_call", output_to_operand_aliasing={{0}: (8, {}), {1}: (9, {})} | custom-call | flops 1024 | bytes 1024 | tf_op jit(solution)/shard_map/stage/pallas_call | solution.py:93
  69.7 4.1 %unpack.10 = (bf16[16,2048,512]{2,1,0:T(8,128)(2,1)}, bf16[1024,512]{1,0:T(8,128)(2,1)}, bf16[1024,512]{1,0:T(8,128)(2,1)}) custom-call(s32[32]{0:T(128)} %get-tuple-element.126.meta, f32[2048,128]{1,0:T(8,128)} %broadcast_in_dim.28.inverse, bf16[2048,512]{1,0:T(8,128)(2,1)} %collective-permute-done.13.raw.__0_, ...), custom_call_target="tpu_custom_call", output_to_operand_aliasing={{0}: (3, {})} | custom-call | flops 1024 | bytes 1024 | tf_op jit(solution)/shard_map/unpack/pallas_call | solution.py:93
  74.4 4.7 %stage.20 = (bf16[16,2048,512]{2,1,0:T(8,128)(2,1)}, f32[34,256,512]{2,1,0:T(8,128)}) custom-call(s32[32]{0:T(128)} %get-tuple-element.126.meta, s32[34]{0:T(128)} %get-tuple-element.120.lefts, s32[34]{0:T(128)} %get-tuple-element.119.rights, s32[34]{0:T(128)} %get-tuple-element.118.slots, ...), custom_call_target="tpu_custom_call", output_to_operand_aliasing={{0}: (6, {}), {1}: (7, {})} | custom-call | flops 1024 | bytes 1024 | tf_op jit(solution)/shard_map/stage/pallas_call | solution.py:93
  79.1 5.2 %stage.21 = (bf16[16,2048,512]{2,1,0:T(8,128)(2,1)}, f32[34,256,512]{2,1,0:T(8,128)}) custom-call(s32[32]{0:T(128)} %get-tuple-element.126.meta, s32[34]{0:T(128)} %get-tuple-element.120.lefts, s32[34]{0:T(128)} %get-tuple-element.119.rights, s32[34]{0:T(128)} %get-tuple-element.118.slots, ...), custom_call_target="tpu_custom_call", output_to_operand_aliasing={{0}: (8, {}), {1}: (9, {})} | custom-call | flops 1024 | bytes 1024 | tf_op jit(solution)/shard_map/stage/pallas_call | solution.py:93
  85.4 4.0 %unpack.11 = (bf16[16,2048,512]{2,1,0:T(8,128)(2,1)}, bf16[1024,512]{1,0:T(8,128)(2,1)}, bf16[1024,512]{1,0:T(8,128)(2,1)}) custom-call(s32[32]{0:T(128)} %get-tuple-element.126.meta, f32[2048,128]{1,0:T(8,128)} %broadcast_in_dim.28.inverse, bf16[2048,512]{1,0:T(8,128)(2,1)} %collective-permute-done.10.raw, ...), custom_call_target="tpu_custom_call", output_to_operand_aliasing={{0}: (3, {})} | custom-call | flops 1024 | bytes 1024 | tf_op jit(solution)/shard_map/unpack/pallas_call | solution.py:93
  91.1 5.5 %stage.22 = (bf16[16,2048,512]{2,1,0:T(8,128)(2,1)}, f32[34,256,512]{2,1,0:T(8,128)}) custom-call(s32[32]{0:T(128)} %get-tuple-element.126.meta, s32[34]{0:T(128)} %get-tuple-element.120.lefts, s32[34]{0:T(128)} %get-tuple-element.119.rights, s32[34]{0:T(128)} %get-tuple-element.118.slots, ...), custom_call_target="tpu_custom_call", output_to_operand_aliasing={{0}: (6, {}), {1}: (7, {})} | custom-call | flops 1024 | bytes 1024 | tf_op jit(solution)/shard_map/stage/pallas_call | solution.py:93
  96.6 6.2 %stage.23 = (bf16[16,2048,512]{2,1,0:T(8,128)(2,1)}, f32[34,256,512]{2,1,0:T(8,128)}) custom-call(s32[32]{0:T(128)} %get-tuple-element.126.meta, s32[34]{0:T(128)} %get-tuple-element.120.lefts, s32[34]{0:T(128)} %get-tuple-element.119.rights, s32[34]{0:T(128)} %get-tuple-element.118.slots, ...), custom_call_target="tpu_custom_call", output_to_operand_aliasing={{0}: (8, {}), {1}: (9, {})} | custom-call | flops 1024 | bytes 1024 | tf_op jit(solution)/shard_map/stage/pallas_call | solution.py:93
  102.8 7.1 %collective-permute-done.18.raw.__0_ = bf16[2048,512]{1,0:T(8,128)(2,1)} collective-permute-done((bf16[2048,512]{1,0:T(8,128)(2,1)}, bf16[2048,512]{1,0:T(8,128)(2,1)}, u32[]{:S(2)}, u32[]{:S(2)}) %collective-permute-start.18) | collective-permute-done | bytes 2097184 | tf_op jit(solution)/shard_map/ppermute | solution.py:396
  109.9 4.0 %unpack.12 = (bf16[16,2048,512]{2,1,0:T(8,128)(2,1)}, bf16[1024,512]{1,0:T(8,128)(2,1)}, bf16[1024,512]{1,0:T(8,128)(2,1)}) custom-call(s32[32]{0:T(128)} %get-tuple-element.126.meta, f32[2048,128]{1,0:T(8,128)} %broadcast_in_dim.28.inverse, bf16[2048,512]{1,0:T(8,128)(2,1)} %collective-permute-done.18.raw.__0_, ...), custom_call_target="tpu_custom_call", output_to_operand_aliasing={{0}: (3, {})} | custom-call | flops 1024 | bytes 1024 | tf_op jit(solution)/shard_map/unpack/pallas_call | solution.py:93
  115.7 4.4 %stage.24 = (bf16[16,2048,512]{2,1,0:T(8,128)(2,1)}, f32[34,256,512]{2,1,0:T(8,128)}) custom-call(s32[32]{0:T(128)} %get-tuple-element.126.meta, s32[34]{0:T(128)} %get-tuple-element.120.lefts, s32[34]{0:T(128)} %get-tuple-element.119.rights, s32[34]{0:T(128)} %get-tuple-element.118.slots, ...), custom_call_target="tpu_custom_call", output_to_operand_aliasing={{0}: (6, {}), {1}: (7, {})} | custom-call | flops 1024 | bytes 1024 | tf_op jit(solution)/shard_map/stage/pallas_call | solution.py:93
  120.2 5.5 %stage.25 = (bf16[16,2048,512]{2,1,0:T(8,128)(2,1)}, f32[34,256,512]{2,1,0:T(8,128)}) custom-call(s32[32]{0:T(128)} %get-tuple-element.126.meta, s32[34]{0:T(128)} %get-tuple-element.120.lefts, s32[34]{0:T(128)} %get-tuple-element.119.rights, s32[34]{0:T(128)} %get-tuple-element.118.slots, ...), custom_call_target="tpu_custom_call", output_to_operand_aliasing={{0}: (8, {}), {1}: (9, {})} | custom-call | flops 1024 | bytes 1024 | tf_op jit(solution)/shard_map/stage/pallas_call | solution.py:93
  128.1 6.9 %collective-permute-done.11.raw = bf16[2048,512]{1,0:T(8,128)(2,1)} collective-permute-done((bf16[2048,512]{1,0:T(8,128)(2,1)}, bf16[2048,512]{1,0:T(8,128)(2,1)}, u32[]{:S(2)}, u32[]{:S(2)}) %collective-permute-start.11) | collective-permute-done | bytes 2097184 | tf_op jit(solution)/shard_map/ppermute | solution.py:396
  135.0 4.1 %unpack.13 = (bf16[16,2048,512]{2,1,0:T(8,128)(2,1)}, bf16[1024,512]{1,0:T(8,128)(2,1)}, bf16[1024,512]{1,0:T(8,128)(2,1)}) custom-call(s32[32]{0:T(128)} %get-tuple-element.126.meta, f32[2048,128]{1,0:T(8,128)} %broadcast_in_dim.28.inverse, bf16[2048,512]{1,0:T(8,128)(2,1)} %collective-permute-done.11.raw, ...), custom_call_target="tpu_custom_call", output_to_operand_aliasing={{0}: (3, {})} | custom-call | flops 1024 | bytes 1024 | tf_op jit(solution)/shard_map/unpack/pallas_call | solution.py:93
  139.0 3.1 %collective-permute-start.24 = (bf16[1024,512]{1,0:T(8,128)(2,1)}, bf16[1024,512]{1,0:T(8,128)(2,1)}, u32[]{:S(2)}, u32[]{:S(2)}) collective-permute-start(bf16[1024,512]{1,0:T(8,128)(2,1)} %get-tuple-element.95), channel_id=1, source_target_pairs={{0,1},{1,0},{2,3},{3,2},{4,5},{5,4},{6,7},{7,6},{8,9},{9,8},{10,11... | collective-permute-start | bytes 3145736 | tf_op jit(solution)/shard_map/ppermute | solution.py:397
  143.4 4.4 %stage.26 = (bf16[16,2048,512]{2,1,0:T(8,128)(2,1)}, f32[34,256,512]{2,1,0:T(8,128)}) custom-call(s32[32]{0:T(128)} %get-tuple-element.126.meta, s32[34]{0:T(128)} %get-tuple-element.120.lefts, s32[34]{0:T(128)} %get-tuple-element.119.rights, s32[34]{0:T(128)} %get-tuple-element.118.slots, ...), custom_call_target="tpu_custom_call", output_to_operand_aliasing={{0}: (6, {}), {1}: (7, {})} | custom-call | flops 1024 | bytes 1024 | tf_op jit(solution)/shard_map/stage/pallas_call | solution.py:93
  147.8 7.0 %stage.27 = (bf16[16,2048,512]{2,1,0:T(8,128)(2,1)}, f32[34,256,512]{2,1,0:T(8,128)}) custom-call(s32[32]{0:T(128)} %get-tuple-element.126.meta, s32[34]{0:T(128)} %get-tuple-element.120.lefts, s32[34]{0:T(128)} %get-tuple-element.119.rights, s32[34]{0:T(128)} %get-tuple-element.118.slots, ...), custom_call_target="tpu_custom_call", output_to_operand_aliasing={{0}: (8, {}), {1}: (9, {})} | custom-call | flops 1024 | bytes 1024 | tf_op jit(solution)/shard_map/stage/pallas_call | solution.py:93
  156.2 4.0 %unpack.14 = (bf16[16,2048,512]{2,1,0:T(8,128)(2,1)}, bf16[1024,512]{1,0:T(8,128)(2,1)}, bf16[1024,512]{1,0:T(8,128)(2,1)}) custom-call(s32[32]{0:T(128)} %get-tuple-element.126.meta, f32[2048,128]{1,0:T(8,128)} %broadcast_in_dim.28.inverse, bf16[2048,512]{1,0:T(8,128)(2,1)} %collective-permute-done.23.raw, ...), custom_call_target="tpu_custom_call", output_to_operand_aliasing={{0}: (3, {})} | custom-call | flops 1024 | bytes 1024 | tf_op jit(solution)/shard_map/unpack/pallas_call | solution.py:93
  160.8 5.5 %stage.28 = (bf16[16,2048,512]{2,1,0:T(8,128)(2,1)}, f32[34,256,512]{2,1,0:T(8,128)}) custom-call(s32[32]{0:T(128)} %get-tuple-element.126.meta, s32[34]{0:T(128)} %get-tuple-element.120.lefts, s32[34]{0:T(128)} %get-tuple-element.119.rights, s32[34]{0:T(128)} %get-tuple-element.118.slots, ...), custom_call_target="tpu_custom_call", output_to_operand_aliasing={{0}: (6, {}), {1}: (7, {})} | custom-call | flops 1024 | bytes 1024 | tf_op jit(solution)/shard_map/stage/pallas_call | solution.py:93
  166.3 7.8 %stage.29 = (bf16[16,2048,512]{2,1,0:T(8,128)(2,1)}, f32[34,256,512]{2,1,0:T(8,128)}) custom-call(s32[32]{0:T(128)} %get-tuple-element.126.meta, s32[34]{0:T(128)} %get-tuple-element.120.lefts, s32[34]{0:T(128)} %get-tuple-element.119.rights, s32[34]{0:T(128)} %get-tuple-element.118.slots, ...), custom_call_target="tpu_custom_call", output_to_operand_aliasing={{0}: (8, {}), {1}: (9, {})} | custom-call | flops 1024 | bytes 1024 | tf_op jit(solution)/shard_map/stage/pallas_call | solution.py:93
  174.1 4.3 %collective-permute-done.12.raw = bf16[2048,512]{1,0:T(8,128)(2,1)} collective-permute-done((bf16[2048,512]{1,0:T(8,128)(2,1)}, bf16[2048,512]{1,0:T(8,128)(2,1)}, u32[]{:S(2)}, u32[]{:S(2)}) %collective-permute-start.12) | collective-permute-done | bytes 2097184 | tf_op jit(solution)/shard_map/ppermute | solution.py:396
  178.3 4.1 %unpack.15 = (bf16[16,2048,512]{2,1,0:T(8,128)(2,1)}, bf16[1024,512]{1,0:T(8,128)(2,1)}, bf16[1024,512]{1,0:T(8,128)(2,1)}) custom-call(s32[32]{0:T(128)} %get-tuple-element.126.meta, f32[2048,128]{1,0:T(8,128)} %broadcast_in_dim.28.inverse, bf16[2048,512]{1,0:T(8,128)(2,1)} %collective-permute-done.12.raw, ...), custom_call_target="tpu_custom_call", output_to_operand_aliasing={{0}: (3, {})} | custom-call | flops 1024 | bytes 1024 | tf_op jit(solution)/shard_map/unpack/pallas_call | solution.py:93
  183.0 7.0 %stage.30 = (bf16[16,2048,512]{2,1,0:T(8,128)(2,1)}, f32[34,256,512]{2,1,0:T(8,128)}) custom-call(s32[32]{0:T(128)} %get-tuple-element.126.meta, s32[34]{0:T(128)} %get-tuple-element.120.lefts, s32[34]{0:T(128)} %get-tuple-element.119.rights, s32[34]{0:T(128)} %get-tuple-element.118.slots, ...), custom_call_target="tpu_custom_call", output_to_operand_aliasing={{0}: (6, {}), {1}: (7, {})} | custom-call | flops 1024 | bytes 1024 | tf_op jit(solution)/shard_map/stage/pallas_call | solution.py:93
  190.1 8.5 %stage.31 = (bf16[16,2048,512]{2,1,0:T(8,128)(2,1)}, f32[34,256,512]{2,1,0:T(8,128)}) custom-call(s32[32]{0:T(128)} %get-tuple-element.126.meta, s32[34]{0:T(128)} %get-tuple-element.120.lefts, s32[34]{0:T(128)} %get-tuple-element.119.rights, s32[34]{0:T(128)} %get-tuple-element.118.slots, ...), custom_call_target="tpu_custom_call", output_to_operand_aliasing={{0}: (8, {}), {1}: (9, {})} | custom-call | flops 1024 | bytes 1024 | tf_op jit(solution)/shard_map/stage/pallas_call | solution.py:93
  (83 shorter events, 38.9 us)
Async XLA Ops:
  1.3 5.3 %collective-permute-start.6 = (bf16[1024,512]{1,0:T(8,128)(2,1)S(1)}, bf16[1024,512]{1,0:T(8,128)(2,1)S(1)}, u32[]{:S(2)}, u32[]{:S(2)}) collective-permute-start(bf16[1024,512]{1,0:T(8,128)(2,1)S(1)} %constant_dynamic-slice_fusion), channel_id=1, source_target_pairs={{0,1},{1,0},{2,3},{3,2},{4,5},{5,4},{6,7},{7,6},{8,9},{9,8},{10,11... | collective-permute-start | bytes 3145736 | tf_op jit(solution)/shard_map/ppermute | solution.py:397
  4.1 2.5 %collective-permute-start = (f32[1024]{0:T(1024)S(1)}, f32[1024]{0:T(1024)S(1)}, u32[]{:S(2)}, u32[]{:S(2)}) collective-permute-start(f32[1024]{0:T(1024)S(1)} %multiply_reduce_fusion), channel_id=1, source_target_pairs={{0,2},{2,0},{4,6},{6,4},{8,10},{10,8},{12,14},{14,12},{1,3},{3,1},... | collective-permute-start | bytes 12296 | tf_op jit(solution)/shard_map/ppermute | solution.py:405
  6.6 1.0 copy-start.2
  10.0 25.9 %collective-permute-start.7 = (bf16[2048,512]{1,0:T(8,128)(2,1)}, bf16[2048,512]{1,0:T(8,128)(2,1)}, u32[]{:S(2)}, u32[]{:S(2)}) collective-permute-start(bf16[2048,512]{1,0:T(8,128)(2,1)} %own.1.__0_), channel_id=1, source_target_pairs={{0,4},{1,3},{2,6},{3,1},{4,0},{5,9},{6,2},{7,11},{8,12},{9,5},{10,... | collective-permute-start | bytes 6291464 | tf_op jit(solution)/shard_map/ppermute | solution.py:396
  11.7 3.5 %collective-permute-start.1 = (f32[1024]{0:T(1024)S(1)}, f32[1024]{0:T(1024)S(1)}, u32[]{:S(2)}, u32[]{:S(2)}) collective-permute-start(f32[1024]{0:T(1024)S(1)} %add.79), channel_id=1, source_target_pairs={{0,1},{1,0},{2,3},{3,2},{4,5},{5,4},{6,7},{7,6},{8,9},{9,8},{10,11... | collective-permute-start | bytes 12296 | tf_op jit(solution)/shard_map/ppermute | solution.py:397
  15.2 4.9 %collective-permute-start.2 = (f32[2,1024]{1,0:T(2,128)S(1)}, f32[2,1024]{1,0:T(2,128)S(1)}, u32[]{:S(2)}, u32[]{:S(2)}) collective-permute-start(f32[2,1024]{1,0:T(2,128)S(1)} %maximum_select_fusion), channel_id=1, source_target_pairs={{1,5},{3,7},{5,1},{7,3},{9,13},{11,15},{13,9},{15,11},{17,21},{19,... | collective-permute-start | bytes 24584 | tf_op jit(solution)/shard_map/ppermute | solution.py:399
  17.3 5.4 %collective-permute-start.3 = (f32[2,1024]{1,0:T(2,128)S(1)}, f32[2,1024]{1,0:T(2,128)S(1)}, u32[]{:S(2)}, u32[]{:S(2)}) collective-permute-start(f32[2,1024]{1,0:T(2,128)S(1)} %maximum_select_fusion), channel_id=1, source_target_pairs={{1,9},{3,11},{4,13},{6,15},{8,1},{10,3},{13,5},{15,7},{17,25},{19,... | collective-permute-start | bytes 24584 | tf_op jit(solution)/shard_map/ppermute | solution.py:399
  18.6 6.5 %collective-permute-start.4 = (f32[2,1024]{1,0:T(2,128)S(1)}, f32[2,1024]{1,0:T(2,128)S(1)}, u32[]{:S(2)}, u32[]{:S(2)}) collective-permute-start(f32[2,1024]{1,0:T(2,128)S(1)} %maximum_select_fusion), channel_id=1, source_target_pairs={{1,13},{3,15},{4,9},{6,11},{8,5},{10,7},{13,1},{15,3},{17,29},{19,... | collective-permute-start | bytes 24584 | tf_op jit(solution)/shard_map/ppermute | solution.py:399
  25.1 10.8 %copy-start.1 = (f32[2,1024]{1,0:T(2,128)}, f32[2,1024]{1,0:T(2,128)S(1)}, u32[]{:S(2)}) copy-start(f32[2,1024]{1,0:T(2,128)S(1)} %add_add_fusion.__1_) | copy-start | bytes 24580
  25.1 1.4 collective-permute-start.5
  36.0 33.7 %collective-permute-start.13 = (bf16[2048,512]{1,0:T(8,128)(2,1)}, bf16[2048,512]{1,0:T(8,128)(2,1)}, u32[]{:S(2)}, u32[]{:S(2)}) collective-permute-start(bf16[2048,512]{1,0:T(8,128)(2,1)} %keep.4.raw), channel_id=1, source_target_pairs={{1,5},{0,2},{3,7},{2,0},{5,1},{4,8},{7,3},{6,10},{9,13},{8,4},{11,... | collective-permute-start | bytes 6291464 | tf_op jit(solution)/shard_map/ppermute | solution.py:396
  42.2 4.6 %collective-permute-start.8 = (bf16[1024,512]{1,0:T(8,128)(2,1)}, bf16[1024,512]{1,0:T(8,128)(2,1)}, u32[]{:S(2)}, u32[]{:S(2)}) collective-permute-start(bf16[1024,512]{1,0:T(8,128)(2,1)} %get-tuple-element.60), channel_id=1, source_target_pairs={{0,1},{1,0},{2,3},{3,2},{4,5},{5,4},{6,7},{7,6},{8,9},{9,8},{10,11... | collective-permute-start | bytes 3145736 | tf_op jit(solution)/shard_map/ppermute | solution.py:397
  43.8 4.1 %collective-permute-start.9 = (bf16[1024,512]{1,0:T(8,128)(2,1)}, bf16[1024,512]{1,0:T(8,128)(2,1)}, u32[]{:S(2)}, u32[]{:S(2)}) collective-permute-start(bf16[1024,512]{1,0:T(8,128)(2,1)} %get-tuple-element.61), channel_id=1, source_target_pairs={{0,1},{1,0},{2,3},{3,2},{4,5},{5,4},{6,7},{7,6},{8,9},{9,8},{10,11... | collective-permute-start | bytes 3145736 | tf_op jit(solution)/shard_map/ppermute | solution.py:397
  56.4 9.4 %collective-permute-start.14 = (bf16[1024,512]{1,0:T(8,128)(2,1)}, bf16[1024,512]{1,0:T(8,128)(2,1)}, u32[]{:S(2)}, u32[]{:S(2)}) collective-permute-start(bf16[1024,512]{1,0:T(8,128)(2,1)} %get-tuple-element.67), channel_id=1, source_target_pairs={{0,1},{1,0},{2,3},{3,2},{4,5},{5,4},{6,7},{7,6},{8,9},{9,8},{10,11... | collective-permute-start | bytes 3145736 | tf_op jit(solution)/shard_map/ppermute | solution.py:397
  57.1 8.7 %collective-permute-start.15 = (bf16[1024,512]{1,0:T(8,128)(2,1)}, bf16[1024,512]{1,0:T(8,128)(2,1)}, u32[]{:S(2)}, u32[]{:S(2)}) collective-permute-start(bf16[1024,512]{1,0:T(8,128)(2,1)} %get-tuple-element.68), channel_id=1, source_target_pairs={{0,1},{1,0},{2,3},{3,2},{4,5},{5,4},{6,7},{7,6},{8,9},{9,8},{10,11... | collective-permute-start | bytes 3145736 | tf_op jit(solution)/shard_map/ppermute | solution.py:397
  57.2 28.2 %collective-permute-start.10 = (bf16[2048,512]{1,0:T(8,128)(2,1)}, bf16[2048,512]{1,0:T(8,128)(2,1)}, u32[]{:S(2)}, u32[]{:S(2)}) collective-permute-start(bf16[2048,512]{1,0:T(8,128)(2,1)} %keep.5.raw), channel_id=1, source_target_pairs={{1,5},{0,2},{3,7},{2,0},{5,1},{4,8},{7,3},{6,10},{9,13},{8,4},{11,... | collective-permute-start | bytes 6291464 | tf_op jit(solution)/shard_map/ppermute | solution.py:396
  73.8 5.3 %collective-permute-start.16 = (bf16[1024,512]{1,0:T(8,128)(2,1)}, bf16[1024,512]{1,0:T(8,128)(2,1)}, u32[]{:S(2)}, u32[]{:S(2)}) collective-permute-start(bf16[1024,512]{1,0:T(8,128)(2,1)} %get-tuple-element.73), channel_id=1, source_target_pairs={{0,1},{1,0},{2,3},{3,2},{4,5},{5,4},{6,7},{7,6},{8,9},{9,8},{10,11... | collective-permute-start | bytes 3145736 | tf_op jit(solution)/shard_map/ppermute | solution.py:397
  73.9 5.2 %collective-permute-start.17 = (bf16[1024,512]{1,0:T(8,128)(2,1)}, bf16[1024,512]{1,0:T(8,128)(2,1)}, u32[]{:S(2)}, u32[]{:S(2)}) collective-permute-start(bf16[1024,512]{1,0:T(8,128)(2,1)} %get-tuple-element.74), channel_id=1, source_target_pairs={{0,1},{1,0},{2,3},{3,2},{4,5},{5,4},{6,7},{7,6},{8,9},{9,8},{10,11... | collective-permute-start | bytes 3145736 | tf_op jit(solution)/shard_map/ppermute | solution.py:397
  84.3 25.6 %collective-permute-start.18 = (bf16[2048,512]{1,0:T(8,128)(2,1)}, bf16[2048,512]{1,0:T(8,128)(2,1)}, u32[]{:S(2)}, u32[]{:S(2)}) collective-permute-start(bf16[2048,512]{1,0:T(8,128)(2,1)} %keep.6), channel_id=1, source_target_pairs={{0,4},{1,3},{2,6},{3,1},{4,0},{5,9},{6,2},{7,11},{8,12},{9,5},{10,... | collective-permute-start | bytes 6291464 | tf_op jit(solution)/shard_map/ppermute | solution.py:396
  89.4 7.2 %collective-permute-start.19 = (bf16[1024,512]{1,0:T(8,128)(2,1)}, bf16[1024,512]{1,0:T(8,128)(2,1)}, u32[]{:S(2)}, u32[]{:S(2)}) collective-permute-start(bf16[1024,512]{1,0:T(8,128)(2,1)} %get-tuple-element.81), channel_id=1, source_target_pairs={{0,1},{1,0},{2,3},{3,2},{4,5},{5,4},{6,7},{7,6},{8,9},{9,8},{10,11... | collective-permute-start | bytes 3145736 | tf_op jit(solution)/shard_map/ppermute | solution.py:397
  90.9 5.6 %collective-permute-start.20 = (bf16[1024,512]{1,0:T(8,128)(2,1)}, bf16[1024,512]{1,0:T(8,128)(2,1)}, u32[]{:S(2)}, u32[]{:S(2)}) collective-permute-start(bf16[1024,512]{1,0:T(8,128)(2,1)} %get-tuple-element.82), channel_id=1, source_target_pairs={{0,1},{1,0},{2,3},{3,2},{4,5},{5,4},{6,7},{7,6},{8,9},{9,8},{10,11... | collective-permute-start | bytes 3145736 | tf_op jit(solution)/shard_map/ppermute | solution.py:397
  91.0 43.9 %collective-permute-start.11 = (bf16[2048,512]{1,0:T(8,128)(2,1)}, bf16[2048,512]{1,0:T(8,128)(2,1)}, u32[]{:S(2)}, u32[]{:S(2)}) collective-permute-start(bf16[2048,512]{1,0:T(8,128)(2,1)} %collective-permute-done.10.raw), channel_id=1, source_target_pairs={{0,4},{1,3},{2,6},{3,1},{4,0},{5,9},{6,2},{7,11},{8,12},{9,5},{10,... | collective-permute-start | bytes 6291464 | tf_op jit(solution)/shard_map/ppermute | solution.py:396
  113.9 6.3 %collective-permute-start.21 = (bf16[1024,512]{1,0:T(8,128)(2,1)}, bf16[1024,512]{1,0:T(8,128)(2,1)}, u32[]{:S(2)}, u32[]{:S(2)}) collective-permute-start(bf16[1024,512]{1,0:T(8,128)(2,1)} %get-tuple-element.87), channel_id=1, source_target_pairs={{0,1},{1,0},{2,3},{3,2},{4,5},{5,4},{6,7},{7,6},{8,9},{9,8},{10,11... | collective-permute-start | bytes 3145736 | tf_op jit(solution)/shard_map/ppermute | solution.py:397
  115.6 4.5 %collective-permute-start.22 = (bf16[1024,512]{1,0:T(8,128)(2,1)}, bf16[1024,512]{1,0:T(8,128)(2,1)}, u32[]{:S(2)}, u32[]{:S(2)}) collective-permute-start(bf16[1024,512]{1,0:T(8,128)(2,1)} %get-tuple-element.88), channel_id=1, source_target_pairs={{0,1},{1,0},{2,3},{3,2},{4,5},{5,4},{6,7},{7,6},{8,9},{9,8},{10,11... | collective-permute-start | bytes 3145736 | tf_op jit(solution)/shard_map/ppermute | solution.py:397
  125.7 30.5 %collective-permute-start.23 = (bf16[2048,512]{1,0:T(8,128)(2,1)}, bf16[2048,512]{1,0:T(8,128)(2,1)}, u32[]{:S(2)}, u32[]{:S(2)}) collective-permute-start(bf16[2048,512]{1,0:T(8,128)(2,1)} %keep.7), channel_id=1, source_target_pairs={{1,5},{0,2},{3,7},{2,0},{5,1},{4,8},{7,3},{6,10},{9,13},{8,4},{11,... | collective-permute-start | bytes 6291464 | tf_op jit(solution)/shard_map/ppermute | solution.py:396
  139.0 8.8 %collective-permute-start.24 = (bf16[1024,512]{1,0:T(8,128)(2,1)}, bf16[1024,512]{1,0:T(8,128)(2,1)}, u32[]{:S(2)}, u32[]{:S(2)}) collective-permute-start(bf16[1024,512]{1,0:T(8,128)(2,1)} %get-tuple-element.95), channel_id=1, source_target_pairs={{0,1},{1,0},{2,3},{3,2},{4,5},{5,4},{6,7},{7,6},{8,9},{9,8},{10,11... | collective-permute-start | bytes 3145736 | tf_op jit(solution)/shard_map/ppermute | solution.py:397
  142.1 5.7 %collective-permute-start.25 = (bf16[1024,512]{1,0:T(8,128)(2,1)}, bf16[1024,512]{1,0:T(8,128)(2,1)}, u32[]{:S(2)}, u32[]{:S(2)}) collective-permute-start(bf16[1024,512]{1,0:T(8,128)(2,1)} %get-tuple-element.96), channel_id=1, source_target_pairs={{0,1},{1,0},{2,3},{3,2},{4,5},{5,4},{6,7},{7,6},{8,9},{9,8},{10,11... | collective-permute-start | bytes 3145736 | tf_op jit(solution)/shard_map/ppermute | solution.py:397
  142.2 36.1 %collective-permute-start.12 = (bf16[2048,512]{1,0:T(8,128)(2,1)}, bf16[2048,512]{1,0:T(8,128)(2,1)}, u32[]{:S(2)}, u32[]{:S(2)}) collective-permute-start(bf16[2048,512]{1,0:T(8,128)(2,1)} %collective-permute-done.11.raw), channel_id=1, source_target_pairs={{1,5},{0,2},{3,7},{2,0},{5,1},{4,8},{7,3},{6,10},{9,13},{8,4},{11,... | collective-permute-start | bytes 6291464 | tf_op jit(solution)/shard_map/ppermute | solution.py:396
  160.2 6.1 %collective-permute-start.26 = (bf16[1024,512]{1,0:T(8,128)(2,1)}, bf16[1024,512]{1,0:T(8,128)(2,1)}, u32[]{:S(2)}, u32[]{:S(2)}) collective-permute-start(bf16[1024,512]{1,0:T(8,128)(2,1)} %get-tuple-element.101), channel_id=1, source_target_pairs={{0,1},{1,0},{2,3},{3,2},{4,5},{5,4},{6,7},{7,6},{8,9},{9,8},{10,11... | collective-permute-start | bytes 3145736 | tf_op jit(solution)/shard_map/ppermute | solution.py:397
  160.3 6.0 %collective-permute-start.27 = (bf16[1024,512]{1,0:T(8,128)(2,1)}, bf16[1024,512]{1,0:T(8,128)(2,1)}, u32[]{:S(2)}, u32[]{:S(2)}) collective-permute-start(bf16[1024,512]{1,0:T(8,128)(2,1)} %get-tuple-element.102), channel_id=1, source_target_pairs={{0,1},{1,0},{2,3},{3,2},{4,5},{5,4},{6,7},{7,6},{8,9},{9,8},{10,11... | collective-permute-start | bytes 3145736 | tf_op jit(solution)/shard_map/ppermute | solution.py:397
  182.4 7.6 %collective-permute-start.28 = (bf16[1024,512]{1,0:T(8,128)(2,1)}, bf16[1024,512]{1,0:T(8,128)(2,1)}, u32[]{:S(2)}, u32[]{:S(2)}) collective-permute-start(bf16[1024,512]{1,0:T(8,128)(2,1)} %get-tuple-element.108), channel_id=1, source_target_pairs={{0,1},{1,0},{2,3},{3,2},{4,5},{5,4},{6,7},{7,6},{8,9},{9,8},{10,11... | collective-permute-start | bytes 3145736 | tf_op jit(solution)/shard_map/ppermute | solution.py:397
  182.5 7.5 %collective-permute-start.29 = (bf16[1024,512]{1,0:T(8,128)(2,1)}, bf16[1024,512]{1,0:T(8,128)(2,1)}, u32[]{:S(2)}, u32[]{:S(2)}) collective-permute-start(bf16[1024,512]{1,0:T(8,128)(2,1)} %get-tuple-element.109), channel_id=1, source_target_pairs={{0,1},{1,0},{2,3},{3,2},{4,5},{5,4},{6,7},{7,6},{8,9},{9,8},{10,11... | collective-permute-start | bytes 3145736 | tf_op jit(solution)/shard_map/ppermute | solution.py:397
  (1 other events, 1.0 us)
where the time goes:
time: 199 us
  Pallas kernels  120 us (60%)
  waiting for transfers between devices  37.6 us (19%)
  starting transfers between devices  29.3 us (15%)
  local copies, waits for them, and re-layouts  5.71 us (3%)
  other arithmetic  5.55 us (3%)
    pallas_call x29, Pallas kernels, call(): pl.pallas_call(kernel, in_specs=[pl.BlockSpec(memory_space=pltpu.SMEM)] *...  120 us
    ppermute x7, waiting for transfers between devices, grid_body(): slot = lambda k, x: lax.ppermute(x, ('tile', 'example'), slot_pairs(k))  30 us
    ppermute x19, starting transfers between devices, grid_body(): swap = lambda x: lax.ppermute(x, 'example', CORES)  14.3 us
    ppermute x7, starting transfers between devices, grid_body(): slot = lambda k, x: lax.ppermute(x, ('tile', 'example'), slot_pairs(k))  9.02 us
    ppermute x3, waiting for transfers between devices, grid_body(): joint = lambda x, pairs: lax.ppermute(x, ('tile', 'example'), pairs)  5.11 us
    ppermute x3, starting transfers between devices, grid_body(): joint = lambda x, pairs: lax.ppermute(x, ('tile', 'example'), pairs)  4.66 us
  transfers between devices with their start and end apart: 30, of which 12 were waited for; matrix products, arithmetic and copies ran while one was open for 5% of the time, Pallas kernels for 53%

commit v1 on v0

--- a/solution.py
+++ b/solution.py
@@ -116,22 +116,20 @@
     )
 
 
-def own_kernel(place, mine, other, *rest):
+def merge_kernel(place, mine, other, *rest):
     whole, room, arrive, leave = rest[-4:]
     core = place[0]
     rows, stripe = other.shape
     pieces = arrive.shape[0] // 2
     part = rows // pieces
-    column = pl.ds(pl.multiple_of(core * stripe, stripe), stripe)
     copies = []
-    for k, side in enumerate((core, 1 - core)):
+    for k, (source, side) in enumerate(((mine, core), (other, 1 - core))):
         for r in range(pieces):
             at = pl.ds(r * part, part)
             target = pl.ds(pl.multiple_of(side * rows + r * part, part), part)
-            source = mine.at[at, column] if k == 0 else other.at[at]
             spot = pieces * k + r
             copies.append((
-                pltpu.make_async_copy(source, room.at[k, at], arrive.at[spot]),
+                pltpu.make_async_copy(source.at[at], room.at[k, at], arrive.at[spot]),
                 pltpu.make_async_copy(room.at[k, at], whole.at[target], leave.at[spot]),
             ))
     for into, _ in copies:
@@ -143,11 +141,11 @@
         outof.wait()
 
 
-def own_stripe(place, mine, other, after):
+def merge(place, mine, other, after=()):
     rows, stripe = other.shape
     return call(
-        own_kernel,
-        "own",
+        merge_kernel,
+        "merge",
         [place, mine, other],
         1,
         [((2 * rows, stripe), jnp.bfloat16)],
@@ -158,7 +156,6 @@
         ],
         {},
         after,
-        pl.ANY,
     )[0]
 
 
@@ -231,9 +228,10 @@
     return lax.dot_general(left, right, (((0,), (0,)), ((), ())), preferred_element_type=jnp.float32)
 
 
-def stage_kernel(cov_scale, stage, given, last, meta, lefts, rights, slots, spans, noise, *rest):
+def stage_kernel(cov_scale, stage, given, last, keeps, meta, lefts, rights, slots, spans, noise, *rest):
     given = rest[:given]
-    held, out, lbuf, rbuf, noises, outs, zeros, arrive, leave, streamed, noised, stored, fill = rest[-13:]
+    inverse = given[1] if last else None
+    held, out, lbuf, rbuf, scales, noises, outs, zeros, arrive, leave, streamed, noised, stored, fill = rest[-14:]
     _, height, stripe = out.shape
     depth = held.shape[1]
     rows = depth // 2
@@ -243,6 +241,8 @@
     columns = pl.ds(pl.multiple_of(here * height, height), height)
     sides = [pl.ds(h * rows, rows) for h in range(2)]
     sources = given or [held.at[place, side] for side in sides]
+    if last:
+        sources = [given[0].at[side] for side in sides]
     into = [pltpu.make_async_copy(sources[h], rbuf.at[0, sides[h]], arrive.at[h]) for h in range(2)]
     outof = [pltpu.make_async_copy(rbuf.at[0, side], held.at[place, side], leave.at[h]) for h, side in enumerate(sides)]
 
@@ -284,14 +284,27 @@
             zeros[...] = jnp.zeros_like(zeros)
             pl.loop(0, dead)(lambda e: clear(e).start())
 
-    @pl.when((end > begin) | (len(given) > 0 and not last))
+    @pl.when((end > begin) | keeps)
     def _():
+        factors = pltpu.make_async_copy(inverse, scales, fill) if last else None
+        if last:
+            factors.start()
         for copy in into:
             copy.start()
         pl.loop(begin, jnp.minimum(begin + ahead, end))(lambda e: fetch(e, lambda copy: copy.start()))
+        if last:
+            factors.wait()
         for copy in into:
             copy.wait()
-        if given and not last:
+        if last:
+            part = depth // 8
+
+            @pl.loop(0, 8)
+            def _(r):
+                at = pl.ds(pl.multiple_of(r * part, part), part)
+                rbuf[0, at] = (rbuf[0, at].astype(jnp.float32) * scales[at, :1]).astype(jnp.bfloat16)
+
+        if keeps:
             for copy in outof:
                 copy.start()
 
@@ -301,7 +314,7 @@
             pl.loop(begin, end)(one_tile)
             pl.loop(jnp.maximum(end - behind, begin), end)(lambda e: store(e).wait())
 
-        if given and not last:
+        if keeps:
             for copy in outof:
                 copy.wait()
 
@@ -309,16 +322,17 @@
         pl.when(dead > 0)(lambda: pl.loop(0, dead)(lambda e: clear(e).wait()))
 
 
-def run_stage(cov_scale, stage, halves, meta, table, spans, noise, held, out):
+def run_stage(cov_scale, stage, arrays, meta, table, spans, noise, held, out):
     slots, height, stripe = noise.shape
     stripes, depth = held.shape[:2]
-    given = [meta, *table, spans, noise, *halves, held]
+    final = 2 * len(EVENTS) - 1
+    given = [meta, *table, spans, noise, *arrays, held]
     aliases = {len(given) - 1: 0}
     if out is not None:
         aliases[len(given)] = 1
         given.append(out)
     return call(
-        functools.partial(stage_kernel, cov_scale, stage, len(halves), stage == 2 * len(EVENTS) - 1),
+        functools.partial(stage_kernel, cov_scale, stage, len(arrays), stage >= final - 1, len(arrays) > 0 and stage < final),
         "stage",
         given,
         5,
@@ -326,6 +340,7 @@
         [
             pltpu.VMEM((1 + AHEAD, depth, height), jnp.bfloat16),
             pltpu.VMEM((1 + AHEAD, depth, stripe), jnp.bfloat16),
+            pltpu.VMEM((depth, 128), jnp.float32),
             pltpu.VMEM((AHEAD, height, stripe), jnp.float32),
             pltpu.VMEM((BEHIND, height, stripe), jnp.float32),
             pltpu.VMEM((height, stripe), jnp.float32),
@@ -399,20 +414,26 @@
     joint = lambda x, pairs: lax.ppermute(x, ("tile", "example"), pairs)
     place = core.reshape(1)
 
-    rows_other = swap(lax.dynamic_slice_in_dim(features, (1 - core) * stripe, stripe, 1))
-    values = features.astype(jnp.float32)
+    mine = lax.dynamic_slice_in_dim(features, core * stripe, stripe, 1)
+    first_mine = slot(0, mine)
+    later, _ = lax.optimization_barrier((features, mine))
+    other = swap(lax.dynamic_slice_in_dim(later, (1 - core) * stripe, stripe, 1))
+    first_other = slot(0, other)
+
+    values = later.astype(jnp.float32)
     squares = jnp.sum(values * values, axis=1)
-    squares_y = lax.ppermute(squares, "tile", Y_SWAP)
-    raw = own_stripe(place, features, rows_other, [squares_y])
-    first_sent = slot(0, raw)
-    squares = squares + squares_y
     squares_other = swap(squares)
     both = jnp.where(core == 0, jnp.stack([squares, squares_other]), jnp.stack([squares_other, squares]))
+    both = both + joint(both, [(2 * a, 2 * b) for a, b in Y_SWAP])
+    both = jnp.where(core == 0, both, swap(both))
     norms = both
     for k in (1, 2, 3):
         source = lambda c: 2 * c + (0 if k > 1 and not is_end(c) else 1)
         norms = norms + joint(both, [(source(c), 2 * (c ^ (2 * k)) + 1) for c in range(chips)])
-    [later] = keep([raw], [norms])
+    raw = merge(place, mine, other)
+    first_mine, first_other = keep([first_mine, first_other], [norms])
+    [later] = keep([raw], [first_other])
+    first_sent = merge(place, first_mine, first_other)
     norms = jnp.where(core == 1, norms, swap(norms)).reshape(2 * rows)
     inverse = 1.0 / jnp.maximum(jnp.sqrt(norms), math.sqrt(2.0 * F))
     inverse = jnp.broadcast_to(inverse[:, None], (2 * rows, 128))
@@ -427,12 +448,14 @@
         raw = later if event == "own" else come[event]
         if event in (0, 2, 4):
             come.append(slot(event + 2, raw))
-        held, halves = unpack(k, raw, meta, inverse, shape, held)
-        halves = [swap(x) for x in halves]
-        held, out = run_stage(cov_scale, 2 * k, [], meta, table, spans, noise_tiles, held, out)
-        held, out = run_stage(cov_scale, 2 * k + 1, halves, meta, table, spans, noise_tiles, held, out)
-        if event == "own":
-            [come[0]] = keep([come[0]], [out])
+        if k < len(EVENTS) - 1:
+            held, halves = unpack(k, raw, meta, inverse, shape, held)
+            mine, theirs = [], [swap(x) for x in halves]
+        else:
+            [raw] = keep([raw], [out])
+            mine, theirs = [raw, inverse], [swap(raw), inverse]
+        held, out = run_stage(cov_scale, 2 * k, mine, meta, table, spans, noise_tiles, held, out)
+        held, out = run_stage(cov_scale, 2 * k + 1, theirs, meta, table, spans, noise_tiles, held, out)
         if event in (1, 3):
             [come[event]] = keep([come[event]], [out])
             come.append(slot(event + 2, come[event]))

time: 199 us -> 193 us (0.970)
  the two profiles are of different devices: /device:TPU:19 before, /device:TPU:5 now
where the time goes in v1:
time: 193 us; the launch traced here: 191 us
  Pallas kernels  116 us (60%)
  starting transfers between devices  34.2 us (18%)
  waiting for transfers between devices  27.8 us (14%)
  local copies, waits for them, and re-layouts  6.92 us (4%)
  other arithmetic  4.95 us (3%)
    pallas_call x30, Pallas kernels, call(): pl.pallas_call(kernel, in_specs=[pl.BlockSpec(memory_space=pltpu.SMEM)] *...  116 us
    ppermute x8, waiting for transfers between devices, grid_body(): slot = lambda k, x: lax.ppermute(x, ('tile', 'example'), slot_pairs(k))  19.8 us
    ppermute x19, starting transfers between devices, grid_body(): swap = lambda x: lax.ppermute(x, 'example', CORES)  16.2 us
    ppermute x4, starting transfers between devices, grid_body(): joint = lambda x, pairs: lax.ppermute(x, ('tile', 'example'), pairs)  9.92 us
    ppermute x8, starting transfers between devices, grid_body(): slot = lambda k, x: lax.ppermute(x, ('tile', 'example'), slot_pairs(k))  8.1 us
    ppermute x19, waiting for transfers between devices, grid_body(): swap = lambda x: lax.ppermute(x, 'example', CORES)  4.37 us
  transfers between devices with their start and end apart: 31, of which 11 were waited for; matrix products, arithmetic and copies ran while one was open for 4% of the time, Pallas kernels for 57%

profile of v1, /device:TPU:5, one launch (start us, length us, event | category | flops | bytes accessed | tf_op | source)
XLA Modules:
  0.0 191.0 jit_solution(2810001147703823803)
XLA Ops:
  9.5 4.8 %collective-permute-start.5 = (f32[2,1024]{1,0:T(2,128)S(1)}, f32[2,1024]{1,0:T(2,128)S(1)}, u32[]{:S(2)}, u32[]{:S(2)}) collective-permute-start(f32[2,1024]{1,0:T(2,128)S(1)} %fusion.5), channel_id=1, source_target_pairs={{0,1},{1,0},{2,3},{3,2},{4,5},{5,4},{6,7},{7,6},{8,9},{9,8},{10,11... | collective-permute-start | bytes 24584 | tf_op jit(solution)/shard_map/ppermute | solution.py:412
  17.5 4.4 %collective-permute-start.7 = (f32[2,1024]{1,0:T(2,128)S(1)}, f32[2,1024]{1,0:T(2,128)S(1)}, u32[]{:S(2)}, u32[]{:S(2)}) collective-permute-start(f32[2,1024]{1,0:T(2,128)S(1)} %broadcast_select_fusion), channel_id=1, source_target_pairs={{1,9},{3,11},{4,13},{6,15},{8,1},{10,3},{13,5},{15,7},{17,25},{19,... | collective-permute-start | bytes 24584 | tf_op jit(solution)/shard_map/ppermute | solution.py:414
  21.8 2.6 %collective-permute-start.8 = (f32[2,1024]{1,0:T(2,128)S(1)}, f32[2,1024]{1,0:T(2,128)S(1)}, u32[]{:S(2)}, u32[]{:S(2)}) collective-permute-start(f32[2,1024]{1,0:T(2,128)S(1)} %broadcast_select_fusion), channel_id=1, source_target_pairs={{1,13},{3,15},{4,9},{6,11},{8,5},{10,7},{13,1},{15,3},{17,29},{19,... | collective-permute-start | bytes 24584 | tf_op jit(solution)/shard_map/ppermute | solution.py:414
  24.6 3.6 %collective-permute-done.8 = f32[2,1024]{1,0:T(2,128)S(1)} collective-permute-done((f32[2,1024]{1,0:T(2,128)S(1)}, f32[2,1024]{1,0:T(2,128)S(1)}, u32[]{:S(2)}, u32[]{:S(2)}) %collective-permute-start.8) | collective-permute-done | bytes 8224 | tf_op jit(solution)/shard_map/ppermute | solution.py:414
  29.5 2.4 %merge.3.__0_ = bf16[2048,512]{1,0:T(8,128)(2,1)} custom-call(s32[1]{0:T(128)} %bitcast.4.place, bf16[1024,512]{1,0:T(8,128)(2,1)} %constant_dynamic-slice_fusion.1.mine, bf16[1024,512]{1,0:T(8,128)(2,1)} %collective-permute-done.1.other), custom_call_target="tpu_custom_call" | custom-call | flops 1024 | bytes 1024 | tf_op jit(solution)/shard_map/merge/pallas_call | solution.py:93
  35.0 4.1 %unpack.7 = (bf16[16,2048,512]{2,1,0:T(8,128)(2,1)}, bf16[1024,512]{1,0:T(8,128)(2,1)}, bf16[1024,512]{1,0:T(8,128)(2,1)}) custom-call(s32[32]{0:T(128)} %get-tuple-element.126.meta, f32[2048,128]{1,0:T(8,128)} %broadcast_in_dim.28.inverse.rest_1_, bf16[2048,512]{1,0:T(8,128)(2,1)} %keep.6.raw), custom_call_target="tpu_custom_call" | custom-call | flops 1024 | bytes 1024 | tf_op jit(solution)/shard_map/unpack/pallas_call | solution.py:93
  41.7 2.5 %merge.2.raw = bf16[2048,512]{1,0:T(8,128)(2,1)} custom-call(s32[1]{0:T(128)} %bitcast.4.place, bf16[1024,512]{1,0:T(8,128)(2,1)} %get-tuple-element.61.mine, bf16[1024,512]{1,0:T(8,128)(2,1)} %get-tuple-element.62.other.__1_), custom_call_target="tpu_custom_call" | custom-call | flops 1024 | bytes 1024 | tf_op jit(solution)/shard_map/merge/pallas_call | solution.py:93
  45.1 3.8 %stage.17 = (bf16[16,2048,512]{2,1,0:T(8,128)(2,1)}, f32[34,256,512]{2,1,0:T(8,128)}) custom-call(s32[32]{0:T(128)} %get-tuple-element.126.meta, s32[34]{0:T(128)} %get-tuple-element.120.lefts, s32[34]{0:T(128)} %get-tuple-element.119.rights, s32[34]{0:T(128)} %get-tuple-element.118.slots, ...), custom_call_target="tpu_custom_call", output_to_operand_aliasing={{0}: (8, {}), {1}: (9, {})} | custom-call | flops 1024 | bytes 1024 | tf_op jit(solution)/shard_map/stage/pallas_call | solution.py:93
  48.9 4.0 %unpack.8 = (bf16[16,2048,512]{2,1,0:T(8,128)(2,1)}, bf16[1024,512]{1,0:T(8,128)(2,1)}, bf16[1024,512]{1,0:T(8,128)(2,1)}) custom-call(s32[32]{0:T(128)} %get-tuple-element.126.meta, f32[2048,128]{1,0:T(8,128)} %broadcast_in_dim.28.inverse.rest_1_, bf16[2048,512]{1,0:T(8,128)(2,1)} %merge.2.raw, ...), custom_call_target="tpu_custom_call", output_to_operand_aliasing={{0}: (3, {})} | custom-call | flops 1024 | bytes 1024 | tf_op jit(solution)/shard_map/unpack/pallas_call | solution.py:93
  53.5 3.3 %collective-permute-start.9 = (bf16[2048,512]{1,0:T(8,128)(2,1)}, bf16[2048,512]{1,0:T(8,128)(2,1)}, u32[]{:S(2)}, u32[]{:S(2)}) collective-permute-start(bf16[2048,512]{1,0:T(8,128)(2,1)} %merge.2.raw), channel_id=1, source_target_pairs={{1,5},{0,2},{3,7},{2,0},{5,1},{4,8},{7,3},{6,10},{9,13},{8,4},{11,... | collective-permute-start | bytes 6291464 | tf_op jit(solution)/shard_map/ppermute | solution.py:411
  57.7 4.7 %stage.19 = (bf16[16,2048,512]{2,1,0:T(8,128)(2,1)}, f32[34,256,512]{2,1,0:T(8,128)}) custom-call(s32[32]{0:T(128)} %get-tuple-element.126.meta, s32[34]{0:T(128)} %get-tuple-element.120.lefts, s32[34]{0:T(128)} %get-tuple-element.119.rights, s32[34]{0:T(128)} %get-tuple-element.118.slots, ...), custom_call_target="tpu_custom_call", output_to_operand_aliasing={{0}: (8, {}), {1}: (9, {})} | custom-call | flops 1024 | bytes 1024 | tf_op jit(solution)/shard_map/stage/pallas_call | solution.py:93
  62.4 4.1 %unpack.9 = (bf16[16,2048,512]{2,1,0:T(8,128)(2,1)}, bf16[1024,512]{1,0:T(8,128)(2,1)}, bf16[1024,512]{1,0:T(8,128)(2,1)}) custom-call(s32[32]{0:T(128)} %get-tuple-element.126.meta, f32[2048,128]{1,0:T(8,128)} %broadcast_in_dim.28.inverse.rest_1_, bf16[2048,512]{1,0:T(8,128)(2,1)} %collective-permute-done.13.raw.__0_, ...), custom_call_target="tpu_custom_call", output_to_operand_aliasing={{0}: (3, {})} | custom-call | flops 1024 | bytes 1024 | tf_op jit(solution)/shard_map/unpack/pallas_call | solution.py:93
  68.1 6.5 %stage.20 = (bf16[16,2048,512]{2,1,0:T(8,128)(2,1)}, f32[34,256,512]{2,1,0:T(8,128)}) custom-call(s32[32]{0:T(128)} %get-tuple-element.126.meta, s32[34]{0:T(128)} %get-tuple-element.120.lefts, s32[34]{0:T(128)} %get-tuple-element.119.rights, s32[34]{0:T(128)} %get-tuple-element.118.slots, ...), custom_call_target="tpu_custom_call", output_to_operand_aliasing={{0}: (6, {}), {1}: (7, {})} | custom-call | flops 1024 | bytes 1024 | tf_op jit(solution)/shard_map/stage/pallas_call | solution.py:93
  74.6 5.2 %stage.21 = (bf16[16,2048,512]{2,1,0:T(8,128)(2,1)}, f32[34,256,512]{2,1,0:T(8,128)}) custom-call(s32[32]{0:T(128)} %get-tuple-element.126.meta, s32[34]{0:T(128)} %get-tuple-element.120.lefts, s32[34]{0:T(128)} %get-tuple-element.119.rights, s32[34]{0:T(128)} %get-tuple-element.118.slots, ...), custom_call_target="tpu_custom_call", output_to_operand_aliasing={{0}: (8, {}), {1}: (9, {})} | custom-call | flops 1024 | bytes 1024 | tf_op jit(solution)/shard_map/stage/pallas_call | solution.py:93
  80.8 4.1 %unpack.10 = (bf16[16,2048,512]{2,1,0:T(8,128)(2,1)}, bf16[1024,512]{1,0:T(8,128)(2,1)}, bf16[1024,512]{1,0:T(8,128)(2,1)}) custom-call(s32[32]{0:T(128)} %get-tuple-element.126.meta, f32[2048,128]{1,0:T(8,128)} %broadcast_in_dim.28.inverse.rest_1_, bf16[2048,512]{1,0:T(8,128)(2,1)} %collective-permute-done.9.raw, ...), custom_call_target="tpu_custom_call", output_to_operand_aliasing={{0}: (3, {})} | custom-call | flops 1024 | bytes 1024 | tf_op jit(solution)/shard_map/unpack/pallas_call | solution.py:93
  86.6 6.3 %stage.22 = (bf16[16,2048,512]{2,1,0:T(8,128)(2,1)}, f32[34,256,512]{2,1,0:T(8,128)}) custom-call(s32[32]{0:T(128)} %get-tuple-element.126.meta, s32[34]{0:T(128)} %get-tuple-element.120.lefts, s32[34]{0:T(128)} %get-tuple-element.119.rights, s32[34]{0:T(128)} %get-tuple-element.118.slots, ...), custom_call_target="tpu_custom_call", output_to_operand_aliasing={{0}: (6, {}), {1}: (7, {})} | custom-call | flops 1024 | bytes 1024 | tf_op jit(solution)/shard_map/stage/pallas_call | solution.py:93
  92.8 6.0 %stage.23 = (bf16[16,2048,512]{2,1,0:T(8,128)(2,1)}, f32[34,256,512]{2,1,0:T(8,128)}) custom-call(s32[32]{0:T(128)} %get-tuple-element.126.meta, s32[34]{0:T(128)} %get-tuple-element.120.lefts, s32[34]{0:T(128)} %get-tuple-element.119.rights, s32[34]{0:T(128)} %get-tuple-element.118.slots, ...), custom_call_target="tpu_custom_call", output_to_operand_aliasing={{0}: (8, {}), {1}: (9, {})} | custom-call | flops 1024 | bytes 1024 | tf_op jit(solution)/shard_map/stage/pallas_call | solution.py:93
  98.8 6.5 %collective-permute-done.20.raw.__0_ = bf16[2048,512]{1,0:T(8,128)(2,1)} collective-permute-done((bf16[2048,512]{1,0:T(8,128)(2,1)}, bf16[2048,512]{1,0:T(8,128)(2,1)}, u32[]{:S(2)}, u32[]{:S(2)}) %collective-permute-start.20) | collective-permute-done | bytes 2097184 | tf_op jit(solution)/shard_map/ppermute | solution.py:411
  105.4 4.0 %unpack.11 = (bf16[16,2048,512]{2,1,0:T(8,128)(2,1)}, bf16[1024,512]{1,0:T(8,128)(2,1)}, bf16[1024,512]{1,0:T(8,128)(2,1)}) custom-call(s32[32]{0:T(128)} %get-tuple-element.126.meta, f32[2048,128]{1,0:T(8,128)} %broadcast_in_dim.28.inverse.rest_1_, bf16[2048,512]{1,0:T(8,128)(2,1)} %collective-permute-done.20.raw.__0_, ...), custom_call_target="tpu_custom_call", output_to_operand_aliasing={{0}: (3, {})} | custom-call | flops 1024 | bytes 1024 | tf_op jit(solution)/shard_map/unpack/pallas_call | solution.py:93
  115.6 4.7 %stage.25 = (bf16[16,2048,512]{2,1,0:T(8,128)(2,1)}, f32[34,256,512]{2,1,0:T(8,128)}) custom-call(s32[32]{0:T(128)} %get-tuple-element.126.meta, s32[34]{0:T(128)} %get-tuple-element.120.lefts, s32[34]{0:T(128)} %get-tuple-element.119.rights, s32[34]{0:T(128)} %get-tuple-element.118.slots, ...), custom_call_target="tpu_custom_call", output_to_operand_aliasing={{0}: (8, {}), {1}: (9, {})} | custom-call | flops 1024 | bytes 1024 | tf_op jit(solution)/shard_map/stage/pallas_call | solution.py:93
  120.4 2.7 %collective-permute-start.25 = (bf16[2048,512]{1,0:T(8,128)(2,1)}, bf16[2048,512]{1,0:T(8,128)(2,1)}, u32[]{:S(2)}, u32[]{:S(2)}) collective-permute-start(bf16[2048,512]{1,0:T(8,128)(2,1)} %keep.8), channel_id=1, source_target_pairs={{1,5},{0,2},{3,7},{2,0},{5,1},{4,8},{7,3},{6,10},{9,13},{8,4},{11,... | collective-permute-start | bytes 6291464 | tf_op jit(solution)/shard_map/ppermute | solution.py:411
  123.1 8.4 %collective-permute-done.10.raw = bf16[2048,512]{1,0:T(8,128)(2,1)} collective-permute-done((bf16[2048,512]{1,0:T(8,128)(2,1)}, bf16[2048,512]{1,0:T(8,128)(2,1)}, u32[]{:S(2)}, u32[]{:S(2)}) %collective-permute-start.10) | collective-permute-done | bytes 2097184 | tf_op jit(solution)/shard_map/ppermute | solution.py:411
  131.5 4.0 %unpack.12 = (bf16[16,2048,512]{2,1,0:T(8,128)(2,1)}, bf16[1024,512]{1,0:T(8,128)(2,1)}, bf16[1024,512]{1,0:T(8,128)(2,1)}) custom-call(s32[32]{0:T(128)} %get-tuple-element.126.meta, f32[2048,128]{1,0:T(8,128)} %broadcast_in_dim.28.inverse.rest_1_, bf16[2048,512]{1,0:T(8,128)(2,1)} %collective-permute-done.10.raw, ...), custom_call_target="tpu_custom_call", output_to_operand_aliasing={{0}: (3, {})} | custom-call | flops 1024 | bytes 1024 | tf_op jit(solution)/shard_map/unpack/pallas_call | solution.py:93
  135.5 3.2 %collective-permute-start.26 = (bf16[1024,512]{1,0:T(8,128)(2,1)}, bf16[1024,512]{1,0:T(8,128)(2,1)}, u32[]{:S(2)}, u32[]{:S(2)}) collective-permute-start(bf16[1024,512]{1,0:T(8,128)(2,1)} %get-tuple-element.98), channel_id=1, source_target_pairs={{0,1},{1,0},{2,3},{3,2},{4,5},{5,4},{6,7},{7,6},{8,9},{9,8},{10,11... | collective-permute-start | bytes 3145736 | tf_op jit(solution)/shard_map/ppermute | solution.py:412
  138.8 5.5 %stage.26 = (bf16[16,2048,512]{2,1,0:T(8,128)(2,1)}, f32[34,256,512]{2,1,0:T(8,128)}) custom-call(s32[32]{0:T(128)} %get-tuple-element.126.meta, s32[34]{0:T(128)} %get-tuple-element.120.lefts, s32[34]{0:T(128)} %get-tuple-element.119.rights, s32[34]{0:T(128)} %get-tuple-element.118.slots, ...), custom_call_target="tpu_custom_call", output_to_operand_aliasing={{0}: (6, {}), {1}: (7, {})} | custom-call | flops 1024 | bytes 1024 | tf_op jit(solution)/shard_map/stage/pallas_call | solution.py:93
  144.3 6.2 %stage.27 = (bf16[16,2048,512]{2,1,0:T(8,128)(2,1)}, f32[34,256,512]{2,1,0:T(8,128)}) custom-call(s32[32]{0:T(128)} %get-tuple-element.126.meta, s32[34]{0:T(128)} %get-tuple-element.120.lefts, s32[34]{0:T(128)} %get-tuple-element.119.rights, s32[34]{0:T(128)} %get-tuple-element.118.slots, ...), custom_call_target="tpu_custom_call", output_to_operand_aliasing={{0}: (8, {}), {1}: (9, {})} | custom-call | flops 1024 | bytes 1024 | tf_op jit(solution)/shard_map/stage/pallas_call | solution.py:93
  152.0 4.0 %unpack.13 = (bf16[16,2048,512]{2,1,0:T(8,128)(2,1)}, bf16[1024,512]{1,0:T(8,128)(2,1)}, bf16[1024,512]{1,0:T(8,128)(2,1)}) custom-call(s32[32]{0:T(128)} %get-tuple-element.126.meta, f32[2048,128]{1,0:T(8,128)} %broadcast_in_dim.28.inverse.rest_1_, bf16[2048,512]{1,0:T(8,128)(2,1)} %collective-permute-done.25.raw, ...), custom_call_target="tpu_custom_call", output_to_operand_aliasing={{0}: (3, {})} | custom-call | flops 1024 | bytes 1024 | tf_op jit(solution)/shard_map/unpack/pallas_call | solution.py:93
  156.5 7.2 %stage.28 = (bf16[16,2048,512]{2,1,0:T(8,128)(2,1)}, f32[34,256,512]{2,1,0:T(8,128)}) custom-call(s32[32]{0:T(128)} %get-tuple-element.126.meta, s32[34]{0:T(128)} %get-tuple-element.120.lefts, s32[34]{0:T(128)} %get-tuple-element.119.rights, s32[34]{0:T(128)} %get-tuple-element.118.slots, ...), custom_call_target="tpu_custom_call", output_to_operand_aliasing={{0}: (6, {}), {1}: (7, {})} | custom-call | flops 1024 | bytes 1024 | tf_op jit(solution)/shard_map/stage/pallas_call | solution.py:93
  163.7 7.9 %stage.29 = (bf16[16,2048,512]{2,1,0:T(8,128)(2,1)}, f32[34,256,512]{2,1,0:T(8,128)}) custom-call(s32[32]{0:T(128)} %get-tuple-element.126.meta, s32[34]{0:T(128)} %get-tuple-element.120.lefts, s32[34]{0:T(128)} %get-tuple-element.119.rights, s32[34]{0:T(128)} %get-tuple-element.118.slots, ...), custom_call_target="tpu_custom_call", output_to_operand_aliasing={{0}: (8, {}), {1}: (9, {})} | custom-call | flops 1024 | bytes 1024 | tf_op jit(solution)/shard_map/stage/pallas_call | solution.py:93
  171.7 2.5 %collective-permute-done.11.__0_ = bf16[2048,512]{1,0:T(8,128)(2,1)} collective-permute-done((bf16[2048,512]{1,0:T(8,128)(2,1)}, bf16[2048,512]{1,0:T(8,128)(2,1)}, u32[]{:S(2)}, u32[]{:S(2)}) %collective-permute-start.11) | collective-permute-done | bytes 2097184 | tf_op jit(solution)/shard_map/ppermute | solution.py:411
  174.1 9.9 %stage.30 = (bf16[16,2048,512]{2,1,0:T(8,128)(2,1)}, f32[34,256,512]{2,1,0:T(8,128)}) custom-call(s32[32]{0:T(128)} %get-tuple-element.126.meta, s32[34]{0:T(128)} %get-tuple-element.120.lefts, s32[34]{0:T(128)} %get-tuple-element.119.rights, s32[34]{0:T(128)} %get-tuple-element.118.slots, ...), custom_call_target="tpu_custom_call", output_to_operand_aliasing={{0}: (8, {}), {1}: (9, {})} | custom-call | flops 1024 | bytes 1024 | tf_op jit(solution)/shard_map/stage/pallas_call | solution.py:93
  184.1 6.7 %stage.31 = (bf16[16,2048,512]{2,1,0:T(8,128)(2,1)}, f32[34,256,512]{2,1,0:T(8,128)}) custom-call(s32[32]{0:T(128)} %get-tuple-element.126.meta, s32[34]{0:T(128)} %get-tuple-element.120.lefts, s32[34]{0:T(128)} %get-tuple-element.119.rights, s32[34]{0:T(128)} %get-tuple-element.118.slots, ...), custom_call_target="tpu_custom_call", output_to_operand_aliasing={{0}: (8, {}), {1}: (9, {})} | custom-call | flops 1024 | bytes 1024 | tf_op jit(solution)/shard_map/stage/pallas_call | solution.py:93
  (84 shorter events, 34.5 us)
Async XLA Ops:
  3.6 5.5 %collective-permute-start.1 = (bf16[1024,512]{1,0:T(8,128)(2,1)S(1)}, bf16[1024,512]{1,0:T(8,128)(2,1)}, u32[]{:S(2)}, u32[]{:S(2)}) collective-permute-start(bf16[1024,512]{1,0:T(8,128)(2,1)S(1)} %constant_dynamic-slice_fusion), channel_id=1, source_target_pairs={{0,1},{1,0},{2,3},{3,2},{4,5},{5,4},{6,7},{7,6},{8,9},{9,8},{10,11... | collective-permute-start | bytes 3145736 | tf_op jit(solution)/shard_map/ppermute | solution.py:412
  6.4 1.2 collective-permute-start.3
  6.5 25.5 %collective-permute-start = (bf16[1024,512]{1,0:T(8,128)(2,1)}, bf16[1024,512]{1,0:T(8,128)(2,1)}, u32[]{:S(2)}, u32[]{:S(2)}) collective-permute-start(bf16[1024,512]{1,0:T(8,128)(2,1)} %constant_dynamic-slice_fusion.1.mine), channel_id=1, source_target_pairs={{0,4},{1,3},{2,6},{3,1},{4,0},{5,9},{6,2},{7,11},{8,12},{9,5},{10,... | collective-permute-start | bytes 3145736 | tf_op jit(solution)/shard_map/ppermute | solution.py:411
  7.6 1.8 collective-permute-start.4
  9.1 23.0 %collective-permute-start.2 = (bf16[1024,512]{1,0:T(8,128)(2,1)}, bf16[1024,512]{1,0:T(8,128)(2,1)}, u32[]{:S(2)}, u32[]{:S(2)}) collective-permute-start(bf16[1024,512]{1,0:T(8,128)(2,1)} %collective-permute-done.1.other), channel_id=1, source_target_pairs={{0,4},{1,3},{2,6},{3,1},{4,0},{5,9},{6,2},{7,11},{8,12},{9,5},{10,... | collective-permute-start | bytes 3145736 | tf_op jit(solution)/shard_map/ppermute | solution.py:411
  9.5 5.7 %collective-permute-start.5 = (f32[2,1024]{1,0:T(2,128)S(1)}, f32[2,1024]{1,0:T(2,128)S(1)}, u32[]{:S(2)}, u32[]{:S(2)}) collective-permute-start(f32[2,1024]{1,0:T(2,128)S(1)} %fusion.5), channel_id=1, source_target_pairs={{0,1},{1,0},{2,3},{3,2},{4,5},{5,4},{6,7},{7,6},{8,9},{9,8},{10,11... | collective-permute-start | bytes 24584 | tf_op jit(solution)/shard_map/ppermute | solution.py:412
  15.2 9.4 %collective-permute-start.6 = (f32[2,1024]{1,0:T(2,128)S(1)}, f32[2,1024]{1,0:T(2,128)S(1)}, u32[]{:S(2)}, u32[]{:S(2)}) collective-permute-start(f32[2,1024]{1,0:T(2,128)S(1)} %broadcast_select_fusion), channel_id=1, source_target_pairs={{1,5},{3,7},{5,1},{7,3},{9,13},{11,15},{13,9},{15,11},{17,21},{19,... | collective-permute-start | bytes 24584 | tf_op jit(solution)/shard_map/ppermute | solution.py:414
  17.5 7.1 %collective-permute-start.7 = (f32[2,1024]{1,0:T(2,128)S(1)}, f32[2,1024]{1,0:T(2,128)S(1)}, u32[]{:S(2)}, u32[]{:S(2)}) collective-permute-start(f32[2,1024]{1,0:T(2,128)S(1)} %broadcast_select_fusion), channel_id=1, source_target_pairs={{1,9},{3,11},{4,13},{6,15},{8,1},{10,3},{13,5},{15,7},{17,25},{19,... | collective-permute-start | bytes 24584 | tf_op jit(solution)/shard_map/ppermute | solution.py:414
  21.8 6.4 %collective-permute-start.8 = (f32[2,1024]{1,0:T(2,128)S(1)}, f32[2,1024]{1,0:T(2,128)S(1)}, u32[]{:S(2)}, u32[]{:S(2)}) collective-permute-start(f32[2,1024]{1,0:T(2,128)S(1)} %broadcast_select_fusion), channel_id=1, source_target_pairs={{1,13},{3,15},{4,9},{6,11},{8,5},{10,7},{13,1},{15,3},{17,29},{19,... | collective-permute-start | bytes 24584 | tf_op jit(solution)/shard_map/ppermute | solution.py:414
  28.2 3.9 %copy-start = (f32[2,1024]{1,0:T(2,128)}, f32[2,1024]{1,0:T(2,128)S(1)}, u32[]{:S(2)}) copy-start(f32[2,1024]{1,0:T(2,128)S(1)} %add_add_fusion.__2_) | copy-start | bytes 24580
  28.2 1.3 collective-permute-start.12
  32.1 30.3 %collective-permute-start.13 = (bf16[2048,512]{1,0:T(8,128)(2,1)}, bf16[2048,512]{1,0:T(8,128)(2,1)}, u32[]{:S(2)}, u32[]{:S(2)}) collective-permute-start(bf16[2048,512]{1,0:T(8,128)(2,1)} %keep.6.raw), channel_id=1, source_target_pairs={{1,5},{0,2},{3,7},{2,0},{5,1},{4,8},{7,3},{6,10},{9,13},{8,4},{11,... | collective-permute-start | bytes 6291464 | tf_op jit(solution)/shard_map/ppermute | solution.py:411
  39.0 6.1 %collective-permute-start.14 = (bf16[1024,512]{1,0:T(8,128)(2,1)}, bf16[1024,512]{1,0:T(8,128)(2,1)}, u32[]{:S(2)}, u32[]{:S(2)}) collective-permute-start(bf16[1024,512]{1,0:T(8,128)(2,1)} %get-tuple-element.63), channel_id=1, source_target_pairs={{0,1},{1,0},{2,3},{3,2},{4,5},{5,4},{6,7},{7,6},{8,9},{9,8},{10,11... | collective-permute-start | bytes 3145736 | tf_op jit(solution)/shard_map/ppermute | solution.py:412
  39.1 6.0 %collective-permute-start.15 = (bf16[1024,512]{1,0:T(8,128)(2,1)}, bf16[1024,512]{1,0:T(8,128)(2,1)}, u32[]{:S(2)}, u32[]{:S(2)}) collective-permute-start(bf16[1024,512]{1,0:T(8,128)(2,1)} %get-tuple-element.64), channel_id=1, source_target_pairs={{0,1},{1,0},{2,3},{3,2},{4,5},{5,4},{6,7},{7,6},{8,9},{9,8},{10,11... | collective-permute-start | bytes 3145736 | tf_op jit(solution)/shard_map/ppermute | solution.py:412
  52.9 4.8 %collective-permute-start.16 = (bf16[1024,512]{1,0:T(8,128)(2,1)}, bf16[1024,512]{1,0:T(8,128)(2,1)}, u32[]{:S(2)}, u32[]{:S(2)}) collective-permute-start(bf16[1024,512]{1,0:T(8,128)(2,1)} %get-tuple-element.69), channel_id=1, source_target_pairs={{0,1},{1,0},{2,3},{3,2},{4,5},{5,4},{6,7},{7,6},{8,9},{9,8},{10,11... | collective-permute-start | bytes 3145736 | tf_op jit(solution)/shard_map/ppermute | solution.py:412
  53.1 4.6 %collective-permute-start.17 = (bf16[1024,512]{1,0:T(8,128)(2,1)}, bf16[1024,512]{1,0:T(8,128)(2,1)}, u32[]{:S(2)}, u32[]{:S(2)}) collective-permute-start(bf16[1024,512]{1,0:T(8,128)(2,1)} %get-tuple-element.70), channel_id=1, source_target_pairs={{0,1},{1,0},{2,3},{3,2},{4,5},{5,4},{6,7},{7,6},{8,9},{9,8},{10,11... | collective-permute-start | bytes 3145736 | tf_op jit(solution)/shard_map/ppermute | solution.py:412
  53.5 27.3 %collective-permute-start.9 = (bf16[2048,512]{1,0:T(8,128)(2,1)}, bf16[2048,512]{1,0:T(8,128)(2,1)}, u32[]{:S(2)}, u32[]{:S(2)}) collective-permute-start(bf16[2048,512]{1,0:T(8,128)(2,1)} %merge.2.raw), channel_id=1, source_target_pairs={{1,5},{0,2},{3,7},{2,0},{5,1},{4,8},{7,3},{6,10},{9,13},{8,4},{11,... | collective-permute-start | bytes 6291464 | tf_op jit(solution)/shard_map/ppermute | solution.py:411
  66.5 8.1 %collective-permute-start.18 = (bf16[1024,512]{1,0:T(8,128)(2,1)}, bf16[1024,512]{1,0:T(8,128)(2,1)}, u32[]{:S(2)}, u32[]{:S(2)}) collective-permute-start(bf16[1024,512]{1,0:T(8,128)(2,1)} %get-tuple-element.76), channel_id=1, source_target_pairs={{0,1},{1,0},{2,3},{3,2},{4,5},{5,4},{6,7},{7,6},{8,9},{9,8},{10,11... | collective-permute-start | bytes 3145736 | tf_op jit(solution)/shard_map/ppermute | solution.py:412
  68.0 6.6 %collective-permute-start.19 = (bf16[1024,512]{1,0:T(8,128)(2,1)}, bf16[1024,512]{1,0:T(8,128)(2,1)}, u32[]{:S(2)}, u32[]{:S(2)}) collective-permute-start(bf16[1024,512]{1,0:T(8,128)(2,1)} %get-tuple-element.77), channel_id=1, source_target_pairs={{0,1},{1,0},{2,3},{3,2},{4,5},{5,4},{6,7},{7,6},{8,9},{9,8},{10,11... | collective-permute-start | bytes 3145736 | tf_op jit(solution)/shard_map/ppermute | solution.py:412
  79.8 25.6 %collective-permute-start.20 = (bf16[2048,512]{1,0:T(8,128)(2,1)}, bf16[2048,512]{1,0:T(8,128)(2,1)}, u32[]{:S(2)}, u32[]{:S(2)}) collective-permute-start(bf16[2048,512]{1,0:T(8,128)(2,1)} %keep.7), channel_id=1, source_target_pairs={{0,4},{1,3},{2,6},{3,1},{4,0},{5,9},{6,2},{7,11},{8,12},{9,5},{10,... | collective-permute-start | bytes 6291464 | tf_op jit(solution)/shard_map/ppermute | solution.py:411
  84.9 8.0 %collective-permute-start.21 = (bf16[1024,512]{1,0:T(8,128)(2,1)}, bf16[1024,512]{1,0:T(8,128)(2,1)}, u32[]{:S(2)}, u32[]{:S(2)}) collective-permute-start(bf16[1024,512]{1,0:T(8,128)(2,1)} %get-tuple-element.84), channel_id=1, source_target_pairs={{0,1},{1,0},{2,3},{3,2},{4,5},{5,4},{6,7},{7,6},{8,9},{9,8},{10,11... | collective-permute-start | bytes 3145736 | tf_op jit(solution)/shard_map/ppermute | solution.py:412
  86.5 6.4 %collective-permute-start.22 = (bf16[1024,512]{1,0:T(8,128)(2,1)}, bf16[1024,512]{1,0:T(8,128)(2,1)}, u32[]{:S(2)}, u32[]{:S(2)}) collective-permute-start(bf16[1024,512]{1,0:T(8,128)(2,1)} %get-tuple-element.85), channel_id=1, source_target_pairs={{0,1},{1,0},{2,3},{3,2},{4,5},{5,4},{6,7},{7,6},{8,9},{9,8},{10,11... | collective-permute-start | bytes 3145736 | tf_op jit(solution)/shard_map/ppermute | solution.py:412
  86.5 45.0 %collective-permute-start.10 = (bf16[2048,512]{1,0:T(8,128)(2,1)}, bf16[2048,512]{1,0:T(8,128)(2,1)}, u32[]{:S(2)}, u32[]{:S(2)}) collective-permute-start(bf16[2048,512]{1,0:T(8,128)(2,1)} %collective-permute-done.9.raw), channel_id=1, source_target_pairs={{0,4},{1,3},{2,6},{3,1},{4,0},{5,9},{6,2},{7,11},{8,12},{9,5},{10,... | collective-permute-start | bytes 6291464 | tf_op jit(solution)/shard_map/ppermute | solution.py:411
  109.4 4.7 %collective-permute-start.23 = (bf16[1024,512]{1,0:T(8,128)(2,1)}, bf16[1024,512]{1,0:T(8,128)(2,1)}, u32[]{:S(2)}, u32[]{:S(2)}) collective-permute-start(bf16[1024,512]{1,0:T(8,128)(2,1)} %get-tuple-element.90), channel_id=1, source_target_pairs={{0,1},{1,0},{2,3},{3,2},{4,5},{5,4},{6,7},{7,6},{8,9},{9,8},{10,11... | collective-permute-start | bytes 3145736 | tf_op jit(solution)/shard_map/ppermute | solution.py:412
  111.5 4.1 %collective-permute-start.24 = (bf16[1024,512]{1,0:T(8,128)(2,1)}, bf16[1024,512]{1,0:T(8,128)(2,1)}, u32[]{:S(2)}, u32[]{:S(2)}) collective-permute-start(bf16[1024,512]{1,0:T(8,128)(2,1)} %get-tuple-element.91), channel_id=1, source_target_pairs={{0,1},{1,0},{2,3},{3,2},{4,5},{5,4},{6,7},{7,6},{8,9},{9,8},{10,11... | collective-permute-start | bytes 3145736 | tf_op jit(solution)/shard_map/ppermute | solution.py:412
  120.4 31.6 %collective-permute-start.25 = (bf16[2048,512]{1,0:T(8,128)(2,1)}, bf16[2048,512]{1,0:T(8,128)(2,1)}, u32[]{:S(2)}, u32[]{:S(2)}) collective-permute-start(bf16[2048,512]{1,0:T(8,128)(2,1)} %keep.8), channel_id=1, source_target_pairs={{1,5},{0,2},{3,7},{2,0},{5,1},{4,8},{7,3},{6,10},{9,13},{8,4},{11,... | collective-permute-start | bytes 6291464 | tf_op jit(solution)/shard_map/ppermute | solution.py:411
  135.5 8.8 %collective-permute-start.26 = (bf16[1024,512]{1,0:T(8,128)(2,1)}, bf16[1024,512]{1,0:T(8,128)(2,1)}, u32[]{:S(2)}, u32[]{:S(2)}) collective-permute-start(bf16[1024,512]{1,0:T(8,128)(2,1)} %get-tuple-element.98), channel_id=1, source_target_pairs={{0,1},{1,0},{2,3},{3,2},{4,5},{5,4},{6,7},{7,6},{8,9},{9,8},{10,11... | collective-permute-start | bytes 3145736 | tf_op jit(solution)/shard_map/ppermute | solution.py:412
  138.7 5.6 %collective-permute-start.27 = (bf16[1024,512]{1,0:T(8,128)(2,1)}, bf16[1024,512]{1,0:T(8,128)(2,1)}, u32[]{:S(2)}, u32[]{:S(2)}) collective-permute-start(bf16[1024,512]{1,0:T(8,128)(2,1)} %get-tuple-element.99), channel_id=1, source_target_pairs={{0,1},{1,0},{2,3},{3,2},{4,5},{5,4},{6,7},{7,6},{8,9},{9,8},{10,11... | collective-permute-start | bytes 3145736 | tf_op jit(solution)/shard_map/ppermute | solution.py:412
  138.8 35.4 %collective-permute-start.11 = (bf16[2048,512]{1,0:T(8,128)(2,1)}, bf16[2048,512]{1,0:T(8,128)(2,1)}, u32[]{:S(2)}, u32[]{:S(2)}) collective-permute-start(bf16[2048,512]{1,0:T(8,128)(2,1)} %collective-permute-done.10.raw), channel_id=1, source_target_pairs={{1,5},{0,2},{3,7},{2,0},{5,1},{4,8},{7,3},{6,10},{9,13},{8,4},{11,... | collective-permute-start | bytes 6291464 | tf_op jit(solution)/shard_map/ppermute | solution.py:411
  155.9 7.8 %collective-permute-start.28 = (bf16[1024,512]{1,0:T(8,128)(2,1)}, bf16[1024,512]{1,0:T(8,128)(2,1)}, u32[]{:S(2)}, u32[]{:S(2)}) collective-permute-start(bf16[1024,512]{1,0:T(8,128)(2,1)} %get-tuple-element.104), channel_id=1, source_target_pairs={{0,1},{1,0},{2,3},{3,2},{4,5},{5,4},{6,7},{7,6},{8,9},{9,8},{10,11... | collective-permute-start | bytes 3145736 | tf_op jit(solution)/shard_map/ppermute | solution.py:412
  156.0 7.7 %collective-permute-start.29 = (bf16[1024,512]{1,0:T(8,128)(2,1)}, bf16[1024,512]{1,0:T(8,128)(2,1)}, u32[]{:S(2)}, u32[]{:S(2)}) collective-permute-start(bf16[1024,512]{1,0:T(8,128)(2,1)} %get-tuple-element.105), channel_id=1, source_target_pairs={{0,1},{1,0},{2,3},{3,2},{4,5},{5,4},{6,7},{7,6},{8,9},{9,8},{10,11... | collective-permute-start | bytes 3145736 | tf_op jit(solution)/shard_map/ppermute | solution.py:412
  174.1 10.0 %collective-permute-start.30 = (bf16[2048,512]{1,0:T(8,128)(2,1)}, bf16[2048,512]{1,0:T(8,128)(2,1)}, u32[]{:S(2)}, u32[]{:S(2)}) collective-permute-start(bf16[2048,512]{1,0:T(8,128)(2,1)} %keep.9.rest_0_), channel_id=1, source_target_pairs={{0,1},{1,0},{2,3},{3,2},{4,5},{5,4},{6,7},{7,6},{8,9},{9,8},{10,11... | collective-permute-start | bytes 6291464 | tf_op jit(solution)/shard_map/ppermute | solution.py:412

commit v2 on v1

--- a/solution.py
+++ b/solution.py
@@ -159,8 +159,8 @@
     )[0]
 
 
-def unpack_kernel(event, meta, inverse, raw, *rest):
-    held, *halves = rest[-9:-6]
+def unpack_kernel(event, whole, meta, inverse, raw, *rest):
+    held, *halves = rest[-9 - whole : -6 - whole]
     taken, given, scales, arrive, leave, wide = rest[-6:]
     depth = held.shape[1]
     pieces = arrive.shape[0]
@@ -178,10 +178,13 @@
 
     def outof(r):
         half = pieces // 2
-        return [
-            pltpu.make_async_copy(given.at[rows(r)], halves[r // half].at[rows(r % half)], leave.at[2 * r]),
-            pltpu.make_async_copy(given.at[rows(r)], held.at[place, rows(r)], leave.at[2 * r + 1]),
+        copies = [
+            pltpu.make_async_copy(given.at[rows(r)], halves[r // half].at[rows(r % half)], leave.at[3 * r]),
+            pltpu.make_async_copy(given.at[rows(r)], held.at[place, rows(r)], leave.at[3 * r + 1]),
         ]
+        if whole:
+            copies.append(pltpu.make_async_copy(given.at[rows(r)], rest[-7].at[rows(r)], leave.at[3 * r + 2]))
+        return copies
 
     for r in range(pieces):
         for copy in into(r):
@@ -197,7 +200,7 @@
             copy.wait()
 
 
-def unpack(event, raw, meta, inverse, shape, held):
+def unpack(event, whole, raw, meta, inverse, shape, held):
     stripes, depth, stripe = shape
     half = ((depth // 2, stripe), jnp.bfloat16)
     pieces = 8
@@ -205,23 +208,23 @@
     if held is not None:
         aliases[len(given)] = 0
         given.append(held)
-    held, *halves = call(
-        functools.partial(unpack_kernel, event),
+    held, *scaled = call(
+        functools.partial(unpack_kernel, event, whole),
         "unpack",
         given,
         1,
-        [(shape, jnp.bfloat16), half, half],
+        [(shape, jnp.bfloat16), half, half] + [((depth, stripe), jnp.bfloat16)] * whole,
         [
             pltpu.VMEM((depth, stripe), jnp.bfloat16),
             pltpu.VMEM((depth, stripe), jnp.bfloat16),
             pltpu.VMEM(inverse.shape, jnp.float32),
             pltpu.SemaphoreType.DMA((pieces,)),
-            pltpu.SemaphoreType.DMA((2 * pieces,)),
+            pltpu.SemaphoreType.DMA((3 * pieces,)),
             pltpu.SemaphoreType.DMA((pieces,)),
         ],
         aliases,
     )
-    return held, halves
+    return held, scaled
 
 
 def dot(left, right):
@@ -230,8 +233,7 @@
 
 def stage_kernel(cov_scale, stage, given, last, keeps, meta, lefts, rights, slots, spans, noise, *rest):
     given = rest[:given]
-    inverse = given[1] if last else None
-    held, out, lbuf, rbuf, scales, noises, outs, zeros, arrive, leave, streamed, noised, stored, fill = rest[-14:]
+    held, out, lbuf, rbuf, noises, outs, zeros, arrive, leave, streamed, noised, stored, fill = rest[-13:]
     _, height, stripe = out.shape
     depth = held.shape[1]
     rows = depth // 2
@@ -286,24 +288,11 @@
 
     @pl.when((end > begin) | keeps)
     def _():
-        factors = pltpu.make_async_copy(inverse, scales, fill) if last else None
-        if last:
-            factors.start()
         for copy in into:
             copy.start()
         pl.loop(begin, jnp.minimum(begin + ahead, end))(lambda e: fetch(e, lambda copy: copy.start()))
-        if last:
-            factors.wait()
         for copy in into:
             copy.wait()
-        if last:
-            part = depth // 8
-
-            @pl.loop(0, 8)
-            def _(r):
-                at = pl.ds(pl.multiple_of(r * part, part), part)
-                rbuf[0, at] = (rbuf[0, at].astype(jnp.float32) * scales[at, :1]).astype(jnp.bfloat16)
-
         if keeps:
             for copy in outof:
                 copy.start()
@@ -340,7 +329,6 @@
         [
             pltpu.VMEM((1 + AHEAD, depth, height), jnp.bfloat16),
             pltpu.VMEM((1 + AHEAD, depth, stripe), jnp.bfloat16),
-            pltpu.VMEM((depth, 128), jnp.float32),
             pltpu.VMEM((AHEAD, height, stripe), jnp.float32),
             pltpu.VMEM((BEHIND, height, stripe), jnp.float32),
             pltpu.VMEM((height, stripe), jnp.float32),
@@ -426,12 +414,14 @@
     both = jnp.where(core == 0, jnp.stack([squares, squares_other]), jnp.stack([squares_other, squares]))
     both = both + joint(both, [(2 * a, 2 * b) for a, b in Y_SWAP])
     both = jnp.where(core == 0, both, swap(both))
+    last, first_mine = keep([both, first_mine], [])
     norms = both
     for k in (1, 2, 3):
         source = lambda c: 2 * c + (0 if k > 1 and not is_end(c) else 1)
-        norms = norms + joint(both, [(source(c), 2 * (c ^ (2 * k)) + 1) for c in range(chips)])
+        message = both if k < 3 else last
+        norms = norms + joint(message, [(source(c), 2 * (c ^ (2 * k)) + 1) for c in range(chips)])
     raw = merge(place, mine, other)
-    first_mine, first_other = keep([first_mine, first_other], [norms])
+    [first_other] = keep([first_other], [norms])
     [later] = keep([raw], [first_other])
     first_sent = merge(place, first_mine, first_other)
     norms = jnp.where(core == 1, norms, swap(norms)).reshape(2 * rows)
@@ -446,19 +436,24 @@
     held = out = None
     for k, event in enumerate(EVENTS):
         raw = later if event == "own" else come[event]
-        if event in (0, 2, 4):
+        if event in (0, 2):
             come.append(slot(event + 2, raw))
         if k < len(EVENTS) - 1:
-            held, halves = unpack(k, raw, meta, inverse, shape, held)
-            mine, theirs = [], [swap(x) for x in halves]
+            held, scaled = unpack(k, event == 4, raw, meta, inverse, shape, held)
+            mine, theirs = [], [swap(x) for x in scaled[:2]]
+            if event == 4:
+                come.append(slot(6, scaled[2]))
         else:
             [raw] = keep([raw], [out])
-            mine, theirs = [raw, inverse], [swap(raw), inverse]
+            mine, theirs = [raw], [swap(raw)]
         held, out = run_stage(cov_scale, 2 * k, mine, meta, table, spans, noise_tiles, held, out)
+        if event == 1:
+            [come[1]] = keep([come[1]], [out])
+            come.append(slot(3, come[1]))
         held, out = run_stage(cov_scale, 2 * k + 1, theirs, meta, table, spans, noise_tiles, held, out)
-        if event in (1, 3):
-            [come[event]] = keep([come[event]], [out])
-            come.append(slot(event + 2, come[event]))
+        if event == 3:
+            [come[3]] = keep([come[3]], [out])
+            come.append(slot(5, come[3]))
     return out
 
 

time: 193 us -> 193 us (level)
  waiting for transfers between devices: 27.8 us -> 19.1 us
  starting transfers between devices: 34.2 us -> 39.4 us
  Pallas kernels: 116 us -> 119 us
    ppermute x8, waiting for transfers between devices: 19.8 us -> 14.7 us  [grid_body(): slot = lambda k, x: lax.ppermute(x, ('tile', 'example'), slot_pairs(k))]
    ppermute x19, waiting for transfers between devices: 4.37 us -> 0.99 us  [grid_body(): swap = lambda x: lax.ppermute(x, 'example', CORES)]
    ppermute x19, starting transfers between devices: 16.2 us -> 19.5 us  [grid_body(): swap = lambda x: lax.ppermute(x, 'example', CORES)]
    pallas_call x30 -> x31, Pallas kernels: 116 us -> 119 us  [call(): pl.pallas_call(kernel, in_specs=[pl.BlockSpec(memory_space=pltpu.SMEM)] *...]
    ppermute x8, starting transfers between devices: 8.1 us -> 10 us  [grid_body(): slot = lambda k, x: lax.ppermute(x, ('tile', 'example'), slot_pairs(k))]
  transfers between devices with their start and end apart: 31 -> 31, of which waited for: 11 -> 7; matrix products, arithmetic and copies ran while one was open for 4% -> 5% of each run, Pallas kernels for 57% -> 58%
where the time goes in v2:
time: 193 us; the launch traced here: 190 us
  Pallas kernels  119 us (62%)
  starting transfers between devices  39.4 us (20%)
  waiting for transfers between devices  19.1 us (10%)
  local copies, waits for them, and re-layouts  7.01 us (4%)
  other arithmetic  4.96 us (3%)
    pallas_call x31, Pallas kernels, call(): pl.pallas_call(kernel, in_specs=[pl.BlockSpec(memory_space=pltpu.SMEM)] *...  119 us
    ppermute x19, starting transfers between devices, grid_body(): swap = lambda x: lax.ppermute(x, 'example', CORES)  19.5 us
    ppermute x8, waiting for transfers between devices, grid_body(): slot = lambda k, x: lax.ppermute(x, ('tile', 'example'), slot_pairs(k))  14.7 us
    ppermute x8, starting transfers between devices, grid_body(): slot = lambda k, x: lax.ppermute(x, ('tile', 'example'), slot_pairs(k))  10 us
    ppermute x4, starting transfers between devices, grid_body(): joint = lambda x, pairs: lax.ppermute(x, ('tile', 'example'), pairs)  9.92 us
  transfers between devices with their start and end apart: 31, of which 7 were waited for; matrix products, arithmetic and copies ran while one was open for 5% of the time, Pallas kernels for 58%

profile of v2, /device:TPU:5, one launch (start us, length us, event | category | flops | bytes accessed | tf_op | source)
XLA Modules:
  0.0 190.2 jit_solution(3512939700302741008)
XLA Ops:
  10.1 4.4 %collective-permute-start.2 = (f32[2,1024]{1,0:T(2,128)S(1)}, f32[2,1024]{1,0:T(2,128)S(1)}, u32[]{:S(2)}, u32[]{:S(2)}) collective-permute-start(f32[2,1024]{1,0:T(2,128)S(1)} %fusion.5), channel_id=1, source_target_pairs={{0,1},{1,0},{2,3},{3,2},{4,5},{5,4},{6,7},{7,6},{8,9},{9,8},{10,11... | collective-permute-start | bytes 24584 | tf_op jit(solution)/shard_map/ppermute | solution.py:400
  15.9 2.8 %collective-permute-start.3 = (f32[2,1024]{1,0:T(2,128)S(1)}, f32[2,1024]{1,0:T(2,128)S(1)}, u32[]{:S(2)}, u32[]{:S(2)}) collective-permute-start(f32[2,1024]{1,0:T(2,128)S(1)} %broadcast_select_fusion), channel_id=1, source_target_pairs={{1,5},{3,7},{5,1},{7,3},{9,13},{11,15},{13,9},{15,11},{17,21},{19,... | collective-permute-start | bytes 24584 | tf_op jit(solution)/shard_map/ppermute | solution.py:402
  18.8 3.5 %collective-permute-start.4 = (f32[2,1024]{1,0:T(2,128)S(1)}, f32[2,1024]{1,0:T(2,128)S(1)}, u32[]{:S(2)}, u32[]{:S(2)}) collective-permute-start(f32[2,1024]{1,0:T(2,128)S(1)} %broadcast_select_fusion), channel_id=1, source_target_pairs={{1,9},{3,11},{4,13},{6,15},{8,1},{10,3},{13,5},{15,7},{17,25},{19,... | collective-permute-start | bytes 24584 | tf_op jit(solution)/shard_map/ppermute | solution.py:402
  22.3 3.0 %collective-permute-start.6 = (f32[2,1024]{1,0:T(2,128)}, f32[2,1024]{1,0:T(2,128)S(1)}, u32[]{:S(2)}, u32[]{:S(2)}) collective-permute-start(f32[2,1024]{1,0:T(2,128)} %get-tuple-element.62), channel_id=1, source_target_pairs={{1,13},{3,15},{4,9},{6,11},{8,5},{10,7},{13,1},{15,3},{17,29},{19,... | collective-permute-start | bytes 24584 | tf_op jit(solution)/shard_map/ppermute | solution.py:402
  25.4 3.4 %collective-permute-done.6 = f32[2,1024]{1,0:T(2,128)S(1)} collective-permute-done((f32[2,1024]{1,0:T(2,128)}, f32[2,1024]{1,0:T(2,128)S(1)}, u32[]{:S(2)}, u32[]{:S(2)}) %collective-permute-start.6) | collective-permute-done | bytes 8224 | tf_op jit(solution)/shard_map/ppermute | solution.py:402
  30.2 2.4 %merge.3.__0_ = bf16[2048,512]{1,0:T(8,128)(2,1)} custom-call(s32[1]{0:T(128)} %bitcast.4.place, bf16[1024,512]{1,0:T(8,128)(2,1)} %copy-done, bf16[1024,512]{1,0:T(8,128)(2,1)} %collective-permute-done.8.other), custom_call_target="tpu_custom_call" | custom-call | flops 1024 | bytes 1024 | tf_op jit(solution)/shard_map/merge/pallas_call | solution.py:93
  34.1 4.1 %unpack.7 = (bf16[16,2048,512]{2,1,0:T(8,128)(2,1)}, bf16[1024,512]{1,0:T(8,128)(2,1)}, bf16[1024,512]{1,0:T(8,128)(2,1)}) custom-call(s32[32]{0:T(128)} %get-tuple-element.128.meta, f32[2048,128]{1,0:T(8,128)} %broadcast_in_dim.28.inverse, bf16[2048,512]{1,0:T(8,128)(2,1)} %keep.8.raw), custom_call_target="tpu_custom_call" | custom-call | flops 1024 | bytes 1024 | tf_op jit(solution)/shard_map/unpack/pallas_call | solution.py:93
  42.3 2.4 %merge.2.raw = bf16[2048,512]{1,0:T(8,128)(2,1)} custom-call(s32[1]{0:T(128)} %bitcast.4.place, bf16[1024,512]{1,0:T(8,128)(2,1)} %get-tuple-element.63.mine, bf16[1024,512]{1,0:T(8,128)(2,1)} %keep.7.other.__1_), custom_call_target="tpu_custom_call" | custom-call | flops 1024 | bytes 1024 | tf_op jit(solution)/shard_map/merge/pallas_call | solution.py:93
  45.7 3.8 %stage.17 = (bf16[16,2048,512]{2,1,0:T(8,128)(2,1)}, f32[34,256,512]{2,1,0:T(8,128)}) custom-call(s32[32]{0:T(128)} %get-tuple-element.128.meta, s32[34]{0:T(128)} %get-tuple-element.122.lefts, s32[34]{0:T(128)} %get-tuple-element.121.rights, s32[34]{0:T(128)} %get-tuple-element.120.slots, ...), custom_call_target="tpu_custom_call", output_to_operand_aliasing={{0}: (8, {}), {1}: (9, {})} | custom-call | flops 1024 | bytes 1024 | tf_op jit(solution)/shard_map/stage/pallas_call | solution.py:93
  49.4 4.1 %unpack.8 = (bf16[16,2048,512]{2,1,0:T(8,128)(2,1)}, bf16[1024,512]{1,0:T(8,128)(2,1)}, bf16[1024,512]{1,0:T(8,128)(2,1)}) custom-call(s32[32]{0:T(128)} %get-tuple-element.128.meta, f32[2048,128]{1,0:T(8,128)} %broadcast_in_dim.28.inverse, bf16[2048,512]{1,0:T(8,128)(2,1)} %merge.2.raw, ...), custom_call_target="tpu_custom_call", output_to_operand_aliasing={{0}: (3, {})} | custom-call | flops 1024 | bytes 1024 | tf_op jit(solution)/shard_map/unpack/pallas_call | solution.py:93
  54.2 5.2 %stage.18 = (bf16[16,2048,512]{2,1,0:T(8,128)(2,1)}, f32[34,256,512]{2,1,0:T(8,128)}) custom-call(s32[32]{0:T(128)} %get-tuple-element.128.meta, s32[34]{0:T(128)} %get-tuple-element.122.lefts, s32[34]{0:T(128)} %get-tuple-element.121.rights, s32[34]{0:T(128)} %get-tuple-element.120.slots, ...), custom_call_target="tpu_custom_call", output_to_operand_aliasing={{0}: (6, {}), {1}: (7, {})} | custom-call | flops 1024 | bytes 1024 | tf_op jit(solution)/shard_map/stage/pallas_call | solution.py:93
  59.4 3.7 %stage.19 = (bf16[16,2048,512]{2,1,0:T(8,128)(2,1)}, f32[34,256,512]{2,1,0:T(8,128)}) custom-call(s32[32]{0:T(128)} %get-tuple-element.128.meta, s32[34]{0:T(128)} %get-tuple-element.122.lefts, s32[34]{0:T(128)} %get-tuple-element.121.rights, s32[34]{0:T(128)} %get-tuple-element.120.slots, ...), custom_call_target="tpu_custom_call", output_to_operand_aliasing={{0}: (8, {}), {1}: (9, {})} | custom-call | flops 1024 | bytes 1024 | tf_op jit(solution)/shard_map/stage/pallas_call | solution.py:93
  63.2 4.1 %unpack.9 = (bf16[16,2048,512]{2,1,0:T(8,128)(2,1)}, bf16[1024,512]{1,0:T(8,128)(2,1)}, bf16[1024,512]{1,0:T(8,128)(2,1)}) custom-call(s32[32]{0:T(128)} %get-tuple-element.128.meta, f32[2048,128]{1,0:T(8,128)} %broadcast_in_dim.28.inverse, bf16[2048,512]{1,0:T(8,128)(2,1)} %collective-permute-done.12.raw.__0_, ...), custom_call_target="tpu_custom_call", output_to_operand_aliasing={{0}: (3, {})} | custom-call | flops 1024 | bytes 1024 | tf_op jit(solution)/shard_map/unpack/pallas_call | solution.py:93
  69.1 6.7 %collective-permute-start.17 = (bf16[2048,512]{1,0:T(8,128)(2,1)}, bf16[2048,512]{1,0:T(8,128)(2,1)}, u32[]{:S(2)}, u32[]{:S(2)}) collective-permute-start(bf16[2048,512]{1,0:T(8,128)(2,1)} %keep.9), channel_id=1, source_target_pairs={{0,4},{1,3},{2,6},{3,1},{4,0},{5,9},{6,2},{7,11},{8,12},{9,5},{10,... | collective-permute-start | bytes 6291464 | tf_op jit(solution)/shard_map/ppermute | solution.py:399
  75.8 6.9 %stage.21 = (bf16[16,2048,512]{2,1,0:T(8,128)(2,1)}, f32[34,256,512]{2,1,0:T(8,128)}) custom-call(s32[32]{0:T(128)} %get-tuple-element.128.meta, s32[34]{0:T(128)} %get-tuple-element.122.lefts, s32[34]{0:T(128)} %get-tuple-element.121.rights, s32[34]{0:T(128)} %get-tuple-element.120.slots, ...), custom_call_target="tpu_custom_call", output_to_operand_aliasing={{0}: (8, {}), {1}: (9, {})} | custom-call | flops 1024 | bytes 1024 | tf_op jit(solution)/shard_map/stage/pallas_call | solution.py:93
  83.2 4.1 %unpack.10 = (bf16[16,2048,512]{2,1,0:T(8,128)(2,1)}, bf16[1024,512]{1,0:T(8,128)(2,1)}, bf16[1024,512]{1,0:T(8,128)(2,1)}) custom-call(s32[32]{0:T(128)} %get-tuple-element.128.meta, f32[2048,128]{1,0:T(8,128)} %broadcast_in_dim.28.inverse, bf16[2048,512]{1,0:T(8,128)(2,1)} %collective-permute-done.10.raw, ...), custom_call_target="tpu_custom_call", output_to_operand_aliasing={{0}: (3, {})} | custom-call | flops 1024 | bytes 1024 | tf_op jit(solution)/shard_map/unpack/pallas_call | solution.py:93
  87.3 3.5 %collective-permute-start.20 = (bf16[1024,512]{1,0:T(8,128)(2,1)}, bf16[1024,512]{1,0:T(8,128)(2,1)}, u32[]{:S(2)}, u32[]{:S(2)}) collective-permute-start(bf16[1024,512]{1,0:T(8,128)(2,1)} %get-tuple-element.84), channel_id=1, source_target_pairs={{0,1},{1,0},{2,3},{3,2},{4,5},{5,4},{6,7},{7,6},{8,9},{9,8},{10,11... | collective-permute-start | bytes 3145736 | tf_op jit(solution)/shard_map/ppermute | solution.py:400
  91.5 5.5 %stage.22 = (bf16[16,2048,512]{2,1,0:T(8,128)(2,1)}, f32[34,256,512]{2,1,0:T(8,128)}) custom-call(s32[32]{0:T(128)} %get-tuple-element.128.meta, s32[34]{0:T(128)} %get-tuple-element.122.lefts, s32[34]{0:T(128)} %get-tuple-element.121.rights, s32[34]{0:T(128)} %get-tuple-element.120.slots, ...), custom_call_target="tpu_custom_call", output_to_operand_aliasing={{0}: (6, {}), {1}: (7, {})} | custom-call | flops 1024 | bytes 1024 | tf_op jit(solution)/shard_map/stage/pallas_call | solution.py:93
  97.1 6.8 %stage.23 = (bf16[16,2048,512]{2,1,0:T(8,128)(2,1)}, f32[34,256,512]{2,1,0:T(8,128)}) custom-call(s32[32]{0:T(128)} %get-tuple-element.128.meta, s32[34]{0:T(128)} %get-tuple-element.122.lefts, s32[34]{0:T(128)} %get-tuple-element.121.rights, s32[34]{0:T(128)} %get-tuple-element.120.slots, ...), custom_call_target="tpu_custom_call", output_to_operand_aliasing={{0}: (8, {}), {1}: (9, {})} | custom-call | flops 1024 | bytes 1024 | tf_op jit(solution)/shard_map/stage/pallas_call | solution.py:93
  104.3 4.1 %unpack.11 = (bf16[16,2048,512]{2,1,0:T(8,128)(2,1)}, bf16[1024,512]{1,0:T(8,128)(2,1)}, bf16[1024,512]{1,0:T(8,128)(2,1)}) custom-call(s32[32]{0:T(128)} %get-tuple-element.128.meta, f32[2048,128]{1,0:T(8,128)} %broadcast_in_dim.28.inverse, bf16[2048,512]{1,0:T(8,128)(2,1)} %collective-permute-done.17.raw.__0_, ...), custom_call_target="tpu_custom_call", output_to_operand_aliasing={{0}: (3, {})} | custom-call | flops 1024 | bytes 1024 | tf_op jit(solution)/shard_map/unpack/pallas_call | solution.py:93
  108.9 5.5 %stage.24 = (bf16[16,2048,512]{2,1,0:T(8,128)(2,1)}, f32[34,256,512]{2,1,0:T(8,128)}) custom-call(s32[32]{0:T(128)} %get-tuple-element.128.meta, s32[34]{0:T(128)} %get-tuple-element.122.lefts, s32[34]{0:T(128)} %get-tuple-element.121.rights, s32[34]{0:T(128)} %get-tuple-element.120.slots, ...), custom_call_target="tpu_custom_call", output_to_operand_aliasing={{0}: (6, {}), {1}: (7, {})} | custom-call | flops 1024 | bytes 1024 | tf_op jit(solution)/shard_map/stage/pallas_call | solution.py:93
  114.4 4.4 %stage.25 = (bf16[16,2048,512]{2,1,0:T(8,128)(2,1)}, f32[34,256,512]{2,1,0:T(8,128)}) custom-call(s32[32]{0:T(128)} %get-tuple-element.128.meta, s32[34]{0:T(128)} %get-tuple-element.122.lefts, s32[34]{0:T(128)} %get-tuple-element.121.rights, s32[34]{0:T(128)} %get-tuple-element.120.slots, ...), custom_call_target="tpu_custom_call", output_to_operand_aliasing={{0}: (8, {}), {1}: (9, {})} | custom-call | flops 1024 | bytes 1024 | tf_op jit(solution)/shard_map/stage/pallas_call | solution.py:93
  119.0 9.2 %collective-permute-done.11.raw = bf16[2048,512]{1,0:T(8,128)(2,1)} collective-permute-done((bf16[2048,512]{1,0:T(8,128)(2,1)}, bf16[2048,512]{1,0:T(8,128)(2,1)}, u32[]{:S(2)}, u32[]{:S(2)}) %collective-permute-start.11) | collective-permute-done | bytes 2097184 | tf_op jit(solution)/shard_map/ppermute | solution.py:399
  128.2 4.8 %unpack.12 = (bf16[16,2048,512]{2,1,0:T(8,128)(2,1)}, bf16[1024,512]{1,0:T(8,128)(2,1)}, bf16[1024,512]{1,0:T(8,128)(2,1)}, bf16[2048,512]{1,0:T(8,128)(2,1)}) custom-call(s32[32]{0:T(128)} %get-tuple-element.128.meta, f32[2048,128]{1,0:T(8,128)} %broadcast_in_dim.28.inverse, ...), custom_call_target="tpu_custom_call", output_to_operand_aliasing={{0}: (3, {})} | custom-call | flops 1024 | bytes 1024 | tf_op jit(solution)/shard_map/unpack/pallas_call | solution.py:93
  137.2 6.2 %stage.26 = (bf16[16,2048,512]{2,1,0:T(8,128)(2,1)}, f32[34,256,512]{2,1,0:T(8,128)}) custom-call(s32[32]{0:T(128)} %get-tuple-element.128.meta, s32[34]{0:T(128)} %get-tuple-element.122.lefts, s32[34]{0:T(128)} %get-tuple-element.121.rights, s32[34]{0:T(128)} %get-tuple-element.120.slots, ...), custom_call_target="tpu_custom_call", output_to_operand_aliasing={{0}: (6, {}), {1}: (7, {})} | custom-call | flops 1024 | bytes 1024 | tf_op jit(solution)/shard_map/stage/pallas_call | solution.py:93
  143.5 4.7 %stage.27 = (bf16[16,2048,512]{2,1,0:T(8,128)(2,1)}, f32[34,256,512]{2,1,0:T(8,128)}) custom-call(s32[32]{0:T(128)} %get-tuple-element.128.meta, s32[34]{0:T(128)} %get-tuple-element.122.lefts, s32[34]{0:T(128)} %get-tuple-element.121.rights, s32[34]{0:T(128)} %get-tuple-element.120.slots, ...), custom_call_target="tpu_custom_call", output_to_operand_aliasing={{0}: (8, {}), {1}: (9, {})} | custom-call | flops 1024 | bytes 1024 | tf_op jit(solution)/shard_map/stage/pallas_call | solution.py:93
  148.2 4.0 %unpack.13 = (bf16[16,2048,512]{2,1,0:T(8,128)(2,1)}, bf16[1024,512]{1,0:T(8,128)(2,1)}, bf16[1024,512]{1,0:T(8,128)(2,1)}) custom-call(s32[32]{0:T(128)} %get-tuple-element.128.meta, f32[2048,128]{1,0:T(8,128)} %broadcast_in_dim.28.inverse, bf16[2048,512]{1,0:T(8,128)(2,1)} %collective-permute-done.25.raw, ...), custom_call_target="tpu_custom_call", output_to_operand_aliasing={{0}: (3, {})} | custom-call | flops 1024 | bytes 1024 | tf_op jit(solution)/shard_map/unpack/pallas_call | solution.py:93
  153.9 5.5 %stage.28 = (bf16[16,2048,512]{2,1,0:T(8,128)(2,1)}, f32[34,256,512]{2,1,0:T(8,128)}) custom-call(s32[32]{0:T(128)} %get-tuple-element.128.meta, s32[34]{0:T(128)} %get-tuple-element.122.lefts, s32[34]{0:T(128)} %get-tuple-element.121.rights, s32[34]{0:T(128)} %get-tuple-element.120.slots, ...), custom_call_target="tpu_custom_call", output_to_operand_aliasing={{0}: (6, {}), {1}: (7, {})} | custom-call | flops 1024 | bytes 1024 | tf_op jit(solution)/shard_map/stage/pallas_call | solution.py:93
  159.4 6.8 %stage.29 = (bf16[16,2048,512]{2,1,0:T(8,128)(2,1)}, f32[34,256,512]{2,1,0:T(8,128)}) custom-call(s32[32]{0:T(128)} %get-tuple-element.128.meta, s32[34]{0:T(128)} %get-tuple-element.122.lefts, s32[34]{0:T(128)} %get-tuple-element.121.rights, s32[34]{0:T(128)} %get-tuple-element.120.slots, ...), custom_call_target="tpu_custom_call", output_to_operand_aliasing={{0}: (8, {}), {1}: (9, {})} | custom-call | flops 1024 | bytes 1024 | tf_op jit(solution)/shard_map/stage/pallas_call | solution.py:93
  166.1 4.5 %collective-permute-done.24.__0_ = bf16[2048,512]{1,0:T(8,128)(2,1)} collective-permute-done((bf16[2048,512]{1,0:T(8,128)(2,1)}, bf16[2048,512]{1,0:T(8,128)(2,1)}, u32[]{:S(2)}, u32[]{:S(2)}) %collective-permute-start.24) | collective-permute-done | bytes 2097184 | tf_op jit(solution)/shard_map/ppermute | solution.py:399
  172.1 10.0 %stage.30 = (bf16[16,2048,512]{2,1,0:T(8,128)(2,1)}, f32[34,256,512]{2,1,0:T(8,128)}) custom-call(s32[32]{0:T(128)} %get-tuple-element.128.meta, s32[34]{0:T(128)} %get-tuple-element.122.lefts, s32[34]{0:T(128)} %get-tuple-element.121.rights, s32[34]{0:T(128)} %get-tuple-element.120.slots, ...), custom_call_target="tpu_custom_call", output_to_operand_aliasing={{0}: (7, {}), {1}: (8, {})} | custom-call | flops 1024 | bytes 1024 | tf_op jit(solution)/shard_map/stage/pallas_call | solution.py:93
  182.1 7.9 %stage.31 = (bf16[16,2048,512]{2,1,0:T(8,128)(2,1)}, f32[34,256,512]{2,1,0:T(8,128)}) custom-call(s32[32]{0:T(128)} %get-tuple-element.128.meta, s32[34]{0:T(128)} %get-tuple-element.122.lefts, s32[34]{0:T(128)} %get-tuple-element.121.rights, s32[34]{0:T(128)} %get-tuple-element.120.slots, ...), custom_call_target="tpu_custom_call", output_to_operand_aliasing={{0}: (7, {}), {1}: (8, {})} | custom-call | flops 1024 | bytes 1024 | tf_op jit(solution)/shard_map/stage/pallas_call | solution.py:93
  (88 shorter events, 31.3 us)
Async XLA Ops:
  3.0 6.8 %collective-permute-start.8 = (bf16[1024,512]{1,0:T(8,128)(2,1)S(1)}, bf16[1024,512]{1,0:T(8,128)(2,1)}, u32[]{:S(2)}, u32[]{:S(2)}) collective-permute-start(bf16[1024,512]{1,0:T(8,128)(2,1)S(1)} %constant_dynamic-slice_fusion), channel_id=1, source_target_pairs={{0,1},{1,0},{2,3},{3,2},{4,5},{5,4},{6,7},{7,6},{8,9},{9,8},{10,11... | collective-permute-start | bytes 3145736 | tf_op jit(solution)/shard_map/ppermute | solution.py:400
  3.7 18.5 %collective-permute-start.5 = (bf16[1024,512]{1,0:T(8,128)(2,1)S(1)}, bf16[1024,512]{1,0:T(8,128)(2,1)}, u32[]{:S(2)}, u32[]{:S(2)}) collective-permute-start(bf16[1024,512]{1,0:T(8,128)(2,1)S(1)} %constant_dynamic-slice_fusion.1.mine), channel_id=1, source_target_pairs={{0,4},{1,3},{2,6},{3,1},{4,0},{5,9},{6,2},{7,11},{8,12},{9,5},{10,... | collective-permute-start | bytes 3145736 | tf_op jit(solution)/shard_map/ppermute | solution.py:399
  5.8 2.5 %collective-permute-start = (f32[1024]{0:T(1024)S(1)}, f32[1024]{0:T(1024)S(1)}, u32[]{:S(2)}, u32[]{:S(2)}) collective-permute-start(f32[1024]{0:T(1024)S(1)} %multiply_reduce_fusion), channel_id=1, source_target_pairs={{0,1},{1,0},{2,3},{3,2},{4,5},{5,4},{6,7},{7,6},{8,9},{9,8},{10,11... | collective-permute-start | bytes 12296 | tf_op jit(solution)/shard_map/ppermute | solution.py:400
  8.4 1.7 collective-permute-start.1
  9.8 22.9 %collective-permute-start.9 = (bf16[1024,512]{1,0:T(8,128)(2,1)}, bf16[1024,512]{1,0:T(8,128)(2,1)}, u32[]{:S(2)}, u32[]{:S(2)}) collective-permute-start(bf16[1024,512]{1,0:T(8,128)(2,1)} %collective-permute-done.8.other), channel_id=1, source_target_pairs={{0,4},{1,3},{2,6},{3,1},{4,0},{5,9},{6,2},{7,11},{8,12},{9,5},{10,... | collective-permute-start | bytes 3145736 | tf_op jit(solution)/shard_map/ppermute | solution.py:399
  10.1 5.3 %collective-permute-start.2 = (f32[2,1024]{1,0:T(2,128)S(1)}, f32[2,1024]{1,0:T(2,128)S(1)}, u32[]{:S(2)}, u32[]{:S(2)}) collective-permute-start(f32[2,1024]{1,0:T(2,128)S(1)} %fusion.5), channel_id=1, source_target_pairs={{0,1},{1,0},{2,3},{3,2},{4,5},{5,4},{6,7},{7,6},{8,9},{9,8},{10,11... | collective-permute-start | bytes 24584 | tf_op jit(solution)/shard_map/ppermute | solution.py:400
  15.9 9.4 %collective-permute-start.3 = (f32[2,1024]{1,0:T(2,128)S(1)}, f32[2,1024]{1,0:T(2,128)S(1)}, u32[]{:S(2)}, u32[]{:S(2)}) collective-permute-start(f32[2,1024]{1,0:T(2,128)S(1)} %broadcast_select_fusion), channel_id=1, source_target_pairs={{1,5},{3,7},{5,1},{7,3},{9,13},{11,15},{13,9},{15,11},{17,21},{19,... | collective-permute-start | bytes 24584 | tf_op jit(solution)/shard_map/ppermute | solution.py:402
  18.8 6.6 %collective-permute-start.4 = (f32[2,1024]{1,0:T(2,128)S(1)}, f32[2,1024]{1,0:T(2,128)S(1)}, u32[]{:S(2)}, u32[]{:S(2)}) collective-permute-start(f32[2,1024]{1,0:T(2,128)S(1)} %broadcast_select_fusion), channel_id=1, source_target_pairs={{1,9},{3,11},{4,13},{6,15},{8,1},{10,3},{13,5},{15,7},{17,25},{19,... | collective-permute-start | bytes 24584 | tf_op jit(solution)/shard_map/ppermute | solution.py:402
  22.3 6.6 %collective-permute-start.6 = (f32[2,1024]{1,0:T(2,128)}, f32[2,1024]{1,0:T(2,128)S(1)}, u32[]{:S(2)}, u32[]{:S(2)}) collective-permute-start(f32[2,1024]{1,0:T(2,128)} %get-tuple-element.62), channel_id=1, source_target_pairs={{1,13},{3,15},{4,9},{6,11},{8,5},{10,7},{13,1},{15,3},{17,29},{19,... | collective-permute-start | bytes 24584 | tf_op jit(solution)/shard_map/ppermute | solution.py:402
  28.9 3.9 %copy-start.1 = (f32[2,1024]{1,0:T(2,128)}, f32[2,1024]{1,0:T(2,128)S(1)}, u32[]{:S(2)}) copy-start(f32[2,1024]{1,0:T(2,128)S(1)} %add_add_fusion.__1_) | copy-start | bytes 24580
  28.9 3.8 %collective-permute-start.7 = (f32[2,1024]{1,0:T(2,128)S(1)}, f32[2,1024]{1,0:T(2,128)S(1)}, u32[]{:S(2)}, u32[]{:S(2)}) collective-permute-start(f32[2,1024]{1,0:T(2,128)S(1)} %add_add_fusion.__1_), channel_id=1, source_target_pairs={{0,1},{1,0},{2,3},{3,2},{4,5},{5,4},{6,7},{7,6},{8,9},{9,8},{10,11... | collective-permute-start | bytes 24584 | tf_op jit(solution)/shard_map/ppermute | solution.py:400
  32.8 30.4 %collective-permute-start.12 = (bf16[2048,512]{1,0:T(8,128)(2,1)}, bf16[2048,512]{1,0:T(8,128)(2,1)}, u32[]{:S(2)}, u32[]{:S(2)}) collective-permute-start(bf16[2048,512]{1,0:T(8,128)(2,1)} %keep.8.raw), channel_id=1, source_target_pairs={{1,5},{0,2},{3,7},{2,0},{5,1},{4,8},{7,3},{6,10},{9,13},{8,4},{11,... | collective-permute-start | bytes 6291464 | tf_op jit(solution)/shard_map/ppermute | solution.py:399
  38.3 7.4 %collective-permute-start.13 = (bf16[1024,512]{1,0:T(8,128)(2,1)}, bf16[1024,512]{1,0:T(8,128)(2,1)}, u32[]{:S(2)}, u32[]{:S(2)}) collective-permute-start(bf16[1024,512]{1,0:T(8,128)(2,1)} %get-tuple-element.64), channel_id=1, source_target_pairs={{0,1},{1,0},{2,3},{3,2},{4,5},{5,4},{6,7},{7,6},{8,9},{9,8},{10,11... | collective-permute-start | bytes 3145736 | tf_op jit(solution)/shard_map/ppermute | solution.py:400
  40.1 5.5 %collective-permute-start.14 = (bf16[1024,512]{1,0:T(8,128)(2,1)}, bf16[1024,512]{1,0:T(8,128)(2,1)}, u32[]{:S(2)}, u32[]{:S(2)}) collective-permute-start(bf16[1024,512]{1,0:T(8,128)(2,1)} %get-tuple-element.65), channel_id=1, source_target_pairs={{0,1},{1,0},{2,3},{3,2},{4,5},{5,4},{6,7},{7,6},{8,9},{9,8},{10,11... | collective-permute-start | bytes 3145736 | tf_op jit(solution)/shard_map/ppermute | solution.py:400
  53.5 5.8 %collective-permute-start.15 = (bf16[1024,512]{1,0:T(8,128)(2,1)}, bf16[1024,512]{1,0:T(8,128)(2,1)}, u32[]{:S(2)}, u32[]{:S(2)}) collective-permute-start(bf16[1024,512]{1,0:T(8,128)(2,1)} %get-tuple-element.70), channel_id=1, source_target_pairs={{0,1},{1,0},{2,3},{3,2},{4,5},{5,4},{6,7},{7,6},{8,9},{9,8},{10,11... | collective-permute-start | bytes 3145736 | tf_op jit(solution)/shard_map/ppermute | solution.py:400
  54.1 5.3 %collective-permute-start.16 = (bf16[1024,512]{1,0:T(8,128)(2,1)}, bf16[1024,512]{1,0:T(8,128)(2,1)}, u32[]{:S(2)}, u32[]{:S(2)}) collective-permute-start(bf16[1024,512]{1,0:T(8,128)(2,1)} %get-tuple-element.71), channel_id=1, source_target_pairs={{0,1},{1,0},{2,3},{3,2},{4,5},{5,4},{6,7},{7,6},{8,9},{9,8},{10,11... | collective-permute-start | bytes 3145736 | tf_op jit(solution)/shard_map/ppermute | solution.py:400
  54.2 29.0 %collective-permute-start.10 = (bf16[2048,512]{1,0:T(8,128)(2,1)}, bf16[2048,512]{1,0:T(8,128)(2,1)}, u32[]{:S(2)}, u32[]{:S(2)}) collective-permute-start(bf16[2048,512]{1,0:T(8,128)(2,1)} %merge.2.raw), channel_id=1, source_target_pairs={{1,5},{0,2},{3,7},{2,0},{5,1},{4,8},{7,3},{6,10},{9,13},{8,4},{11,... | collective-permute-start | bytes 6291464 | tf_op jit(solution)/shard_map/ppermute | solution.py:399
  67.3 8.5 %collective-permute-start.18 = (bf16[1024,512]{1,0:T(8,128)(2,1)}, bf16[1024,512]{1,0:T(8,128)(2,1)}, u32[]{:S(2)}, u32[]{:S(2)}) collective-permute-start(bf16[1024,512]{1,0:T(8,128)(2,1)} %get-tuple-element.80), channel_id=1, source_target_pairs={{0,1},{1,0},{2,3},{3,2},{4,5},{5,4},{6,7},{7,6},{8,9},{9,8},{10,11... | collective-permute-start | bytes 3145736 | tf_op jit(solution)/shard_map/ppermute | solution.py:400
  68.1 7.7 %collective-permute-start.19 = (bf16[1024,512]{1,0:T(8,128)(2,1)}, bf16[1024,512]{1,0:T(8,128)(2,1)}, u32[]{:S(2)}, u32[]{:S(2)}) collective-permute-start(bf16[1024,512]{1,0:T(8,128)(2,1)} %get-tuple-element.81), channel_id=1, source_target_pairs={{0,1},{1,0},{2,3},{3,2},{4,5},{5,4},{6,7},{7,6},{8,9},{9,8},{10,11... | collective-permute-start | bytes 3145736 | tf_op jit(solution)/shard_map/ppermute | solution.py:400
  69.1 35.2 %collective-permute-start.17 = (bf16[2048,512]{1,0:T(8,128)(2,1)}, bf16[2048,512]{1,0:T(8,128)(2,1)}, u32[]{:S(2)}, u32[]{:S(2)}) collective-permute-start(bf16[2048,512]{1,0:T(8,128)(2,1)} %keep.9), channel_id=1, source_target_pairs={{0,4},{1,3},{2,6},{3,1},{4,0},{5,9},{6,2},{7,11},{8,12},{9,5},{10,... | collective-permute-start | bytes 6291464 | tf_op jit(solution)/shard_map/ppermute | solution.py:399
  87.3 9.8 %collective-permute-start.20 = (bf16[1024,512]{1,0:T(8,128)(2,1)}, bf16[1024,512]{1,0:T(8,128)(2,1)}, u32[]{:S(2)}, u32[]{:S(2)}) collective-permute-start(bf16[1024,512]{1,0:T(8,128)(2,1)} %get-tuple-element.84), channel_id=1, source_target_pairs={{0,1},{1,0},{2,3},{3,2},{4,5},{5,4},{6,7},{7,6},{8,9},{9,8},{10,11... | collective-permute-start | bytes 3145736 | tf_op jit(solution)/shard_map/ppermute | solution.py:400
  90.8 6.2 %collective-permute-start.21 = (bf16[1024,512]{1,0:T(8,128)(2,1)}, bf16[1024,512]{1,0:T(8,128)(2,1)}, u32[]{:S(2)}, u32[]{:S(2)}) collective-permute-start(bf16[1024,512]{1,0:T(8,128)(2,1)} %get-tuple-element.85), channel_id=1, source_target_pairs={{0,1},{1,0},{2,3},{3,2},{4,5},{5,4},{6,7},{7,6},{8,9},{9,8},{10,11... | collective-permute-start | bytes 3145736 | tf_op jit(solution)/shard_map/ppermute | solution.py:400
  90.9 37.3 %collective-permute-start.11 = (bf16[2048,512]{1,0:T(8,128)(2,1)}, bf16[2048,512]{1,0:T(8,128)(2,1)}, u32[]{:S(2)}, u32[]{:S(2)}) collective-permute-start(bf16[2048,512]{1,0:T(8,128)(2,1)} %collective-permute-done.10.raw), channel_id=1, source_target_pairs={{0,4},{1,3},{2,6},{3,1},{4,0},{5,9},{6,2},{7,11},{8,12},{9,5},{10,... | collective-permute-start | bytes 6291464 | tf_op jit(solution)/shard_map/ppermute | solution.py:399
  108.3 6.1 %collective-permute-start.22 = (bf16[1024,512]{1,0:T(8,128)(2,1)}, bf16[1024,512]{1,0:T(8,128)(2,1)}, u32[]{:S(2)}, u32[]{:S(2)}) collective-permute-start(bf16[1024,512]{1,0:T(8,128)(2,1)} %get-tuple-element.91), channel_id=1, source_target_pairs={{0,1},{1,0},{2,3},{3,2},{4,5},{5,4},{6,7},{7,6},{8,9},{9,8},{10,11... | collective-permute-start | bytes 3145736 | tf_op jit(solution)/shard_map/ppermute | solution.py:400
  108.4 6.0 %collective-permute-start.23 = (bf16[1024,512]{1,0:T(8,128)(2,1)}, bf16[1024,512]{1,0:T(8,128)(2,1)}, u32[]{:S(2)}, u32[]{:S(2)}) collective-permute-start(bf16[1024,512]{1,0:T(8,128)(2,1)} %get-tuple-element.92), channel_id=1, source_target_pairs={{0,1},{1,0},{2,3},{3,2},{4,5},{5,4},{6,7},{7,6},{8,9},{9,8},{10,11... | collective-permute-start | bytes 3145736 | tf_op jit(solution)/shard_map/ppermute | solution.py:400
  118.9 29.3 %collective-permute-start.25 = (bf16[2048,512]{1,0:T(8,128)(2,1)}, bf16[2048,512]{1,0:T(8,128)(2,1)}, u32[]{:S(2)}, u32[]{:S(2)}) collective-permute-start(bf16[2048,512]{1,0:T(8,128)(2,1)} %keep.10), channel_id=1, source_target_pairs={{1,5},{0,2},{3,7},{2,0},{5,1},{4,8},{7,3},{6,10},{9,13},{8,4},{11,... | collective-permute-start | bytes 6291464 | tf_op jit(solution)/shard_map/ppermute | solution.py:399
  133.0 10.4 %collective-permute-start.26 = (bf16[1024,512]{1,0:T(8,128)(2,1)}, bf16[1024,512]{1,0:T(8,128)(2,1)}, u32[]{:S(2)}, u32[]{:S(2)}) collective-permute-start(bf16[1024,512]{1,0:T(8,128)(2,1)} %get-tuple-element.100), channel_id=1, source_target_pairs={{0,1},{1,0},{2,3},{3,2},{4,5},{5,4},{6,7},{7,6},{8,9},{9,8},{10,11... | collective-permute-start | bytes 3145736 | tf_op jit(solution)/shard_map/ppermute | solution.py:400
  134.8 8.7 %collective-permute-start.27 = (bf16[1024,512]{1,0:T(8,128)(2,1)}, bf16[1024,512]{1,0:T(8,128)(2,1)}, u32[]{:S(2)}, u32[]{:S(2)}) collective-permute-start(bf16[1024,512]{1,0:T(8,128)(2,1)} %get-tuple-element.101), channel_id=1, source_target_pairs={{0,1},{1,0},{2,3},{3,2},{4,5},{5,4},{6,7},{7,6},{8,9},{9,8},{10,11... | collective-permute-start | bytes 3145736 | tf_op jit(solution)/shard_map/ppermute | solution.py:400
  134.9 35.8 %collective-permute-start.24 = (bf16[2048,512]{1,0:T(8,128)(2,1)}, bf16[2048,512]{1,0:T(8,128)(2,1)}, u32[]{:S(2)}, u32[]{:S(2)}) collective-permute-start(bf16[2048,512]{1,0:T(8,128)(2,1)} %get-tuple-element.98), channel_id=1, source_target_pairs={{1,5},{0,2},{3,7},{2,0},{5,1},{4,8},{7,3},{6,10},{9,13},{8,4},{11,... | collective-permute-start | bytes 6291464 | tf_op jit(solution)/shard_map/ppermute | solution.py:399
  152.3 7.1 %collective-permute-start.28 = (bf16[1024,512]{1,0:T(8,128)(2,1)}, bf16[1024,512]{1,0:T(8,128)(2,1)}, u32[]{:S(2)}, u32[]{:S(2)}) collective-permute-start(bf16[1024,512]{1,0:T(8,128)(2,1)} %get-tuple-element.106), channel_id=1, source_target_pairs={{0,1},{1,0},{2,3},{3,2},{4,5},{5,4},{6,7},{7,6},{8,9},{9,8},{10,11... | collective-permute-start | bytes 3145736 | tf_op jit(solution)/shard_map/ppermute | solution.py:400
  153.8 5.6 %collective-permute-start.29 = (bf16[1024,512]{1,0:T(8,128)(2,1)}, bf16[1024,512]{1,0:T(8,128)(2,1)}, u32[]{:S(2)}, u32[]{:S(2)}) collective-permute-start(bf16[1024,512]{1,0:T(8,128)(2,1)} %get-tuple-element.107), channel_id=1, source_target_pairs={{0,1},{1,0},{2,3},{3,2},{4,5},{5,4},{6,7},{7,6},{8,9},{9,8},{10,11... | collective-permute-start | bytes 3145736 | tf_op jit(solution)/shard_map/ppermute | solution.py:400
  170.7 11.4 %collective-permute-start.30 = (bf16[2048,512]{1,0:T(8,128)(2,1)}, bf16[2048,512]{1,0:T(8,128)(2,1)}, u32[]{:S(2)}, u32[]{:S(2)}) collective-permute-start(bf16[2048,512]{1,0:T(8,128)(2,1)} %keep.11.rest_0_), channel_id=1, source_target_pairs={{0,1},{1,0},{2,3},{3,2},{4,5},{5,4},{6,7},{7,6},{8,9},{9,8},{10,11... | collective-permute-start | bytes 6291464 | tf_op jit(solution)/shard_map/ppermute | solution.py:400
  (1 other events, 2.4 us)
